TPU v7x, 32 devices: a whole 2x2x4 slice. The times are simulated.
32 devices in a mesh: rad: 8 (over z, y), lm: 4 (over x, core).
Axes of the slice: x: 2, y: 2, z: 4, core: 2. Of those that a mesh axis runs over, the one named last changes fastest.
Arguments:
- grid_field: bfloat16 [2, 512, 544, 128], P(None, ('rad', 'lm')), may hold values from -6 to 6
- inverses: bfloat16 [2, 64, 512, 512], P(None, ('rad', 'lm')), may hold values from -4 to 4
- slot_blocks: int32 [32, 24], replicated, may hold values from 0 to 544, as said below
- degree_start: int32 [64], replicated, may hold values from 0 to 752, as said below
Outputs:
- new_grid: bfloat16 [2, 512, 544, 128], P(None, ('rad', 'lm'))
- new_slope: bfloat16 [2, 512, 544, 128], P(None, ('rad', 'lm'))
Inputs may be any that keep to these rules, and one draw needn't show every extreme that they name: `slot_blocks`: row d lists the blocks of one degree index below 32 in order, then those of one degree index at or above it in order, then the value 544 (no block). Every block is in exactly one slot. `degree_start`: entry q equals d * 24 + s where slot s of row d of slot_blocks holds the first block of degree index q.
All inputs are finite; a program needn't handle non-finite values.
Results may differ from a plain program's by a relative error of at most 0.0052.
Values may be sent and summed in bfloat16 or wider, within the bound.
No kernel may reach another device: no remote copies, remote signals or barrier semaphores. Data moves between devices by JAX's collectives and lax.ppermute only.
A program may use at most 128 MiB of HBM per device.

v0:
```python
import functools

import jax
import jax.numpy as jnp
import numpy as np
from jax import lax
from jax.experimental import pallas as pl
from jax.experimental.pallas import tpu as pltpu
from jax.sharding import PartitionSpec as P

LMAX1 = 1024
OB = 64
AXES = ("rad", "lm")
PLANE = 8
GROUP = 16

inner_radius = 0.35
shell_depth = 0.65
diffusion_numbers = (0.9, 0.4)


class Sizes:
    def __init__(self, devices, grid_field, inverses, slot_blocks):
        self.devices = devices
        self.fields, self.local, self.blocks, self.width = grid_field.shape
        self.levels = inverses.shape[-1]
        self.capacity = slot_blocks.shape[1]
        self.degrees = 2 * devices
        self.spacing = LMAX1 // self.degrees
        self.group_size = OB * self.degrees // LMAX1
        index = np.arange(self.degrees)
        self.counts = [int(c) for c in index // self.group_size + 1]
        self.starts = [int(s) for s in np.cumsum(self.counts) - self.counts]


def slot_choices(z):
    mean = -(-z.blocks // z.devices)
    return sorted({min(mean + extra, z.capacity) for extra in (1, 2, 3, 4)} | {z.capacity})


def plan_kernel(z, choices, start_ref, choice_ref, place_ref, load_ref, device_ref, next_ref):
    half = z.degrees // 2
    planes = z.devices // PLANE
    owner = [lax.div(start_ref[q], z.capacity) for q in range(z.degrees)]
    for q in range(half, z.degrees):
        load_ref[owner[q]] = start_ref[q] - owner[q] * z.capacity + z.counts[q]
    totals = [sum(load_ref[g * PLANE + e] for e in range(PLANE)) for g in range(planes)]
    most = functools.reduce(jnp.maximum, totals)
    choice = jnp.int32(0)
    slots = jnp.int32(choices[0])
    for i in range(1, len(choices)):
        beyond = most > PLANE * choices[i - 1]
        choice = jnp.where(beyond, i, choice)
        slots = jnp.where(beyond, choices[i], slots)
    choice_ref[0] = choice
    for g in range(planes):
        device_ref[g] = g * PLANE
        next_ref[g] = load_ref[g * PLANE]
    for q in range(z.degrees):
        first = start_ref[q] + owner[q] * (slots - z.capacity)
        for p in range(z.counts[q]):
            place_ref[z.starts[q] + p] = first + p
    for q in range(half, z.degrees):
        if z.counts[half - 1] + z.counts[q] <= choices[0]:
            continue
        plane = lax.div(owner[q], PLANE)
        room = slots - (start_ref[q] - owner[q] * z.capacity)

        def move(p, carry, plane=plane, q=q):
            def full(state):
                return state[1] >= slots

            def advance(state):
                return state[0] + 1, load_ref[state[0] + 1]

            holder, slot = lax.while_loop(full, advance, (device_ref[plane], next_ref[plane]))
            device_ref[plane] = holder
            next_ref[plane] = slot + 1
            place_ref[z.starts[q] + p] = holder * slots + slot
            return carry

        lax.fori_loop(jnp.minimum(room, z.counts[q]), z.counts[q], move, 0)


def plan(z, degree_start, choices):
    smem = pl.BlockSpec(memory_space=pltpu.SMEM)
    planes = z.devices // PLANE
    return pl.pallas_call(
        functools.partial(plan_kernel, z, choices),
        in_specs=[smem],
        out_specs=[smem] * 2,
        out_shape=[
            jax.ShapeDtypeStruct((1,), jnp.int32),
            jax.ShapeDtypeStruct((z.blocks,), jnp.int32),
        ],
        scratch_shapes=[
            pltpu.SMEM((z.devices,), jnp.int32),
            pltpu.SMEM((planes,), jnp.int32),
            pltpu.SMEM((planes,), jnp.int32),
        ],
        name="plan",
    )(degree_start)


def swap(value, axis, bit):
    size = lax.axis_size(axis)
    return lax.ppermute(value, axis, [(i, i ^ bit) for i in range(size)])


def straight_inverses(inverses):
    own = inverses[:, 1]
    return own, swap(own, "lm", 2), swap(own, "rad", 1)


def plane_inverses(own, across, along):
    corner = [swap(across[:1], "rad", 1), swap(along[1:], "lm", 2)]
    even = [own, across, along] + corner
    return even, [swap(value, "lm", 1) for value in even]


def pack_kernel(z, place_ref, field_ref, out_ref, *rest):
    wide_ref = rest[-1]
    pitch = z.blocks + 1
    for level in range(z.local):
        wide_ref[pl.ds(level * pitch, z.blocks), :] = field_ref[0, level].astype(jnp.float32)

    def group(g, carry):
        for k in range(GROUP):
            b = g * GROUP + k
            tile = wide_ref[pl.ds(b, z.local, stride=pitch), :]
            out_ref[place_ref[b]] = tile.astype(jnp.bfloat16)
        return carry

    lax.fori_loop(0, z.blocks // GROUP, group, 0)
    if len(rest) == 1:
        return
    holder_ref = rest[0]

    def clear(k, carry):
        holder_ref[k] = 0
        return carry

    lax.fori_loop(0, z.devices * z.capacity, clear, 0, unroll=8)

    def degree(q, b):
        def block(p, inner):
            holder_ref[place_ref[b + p]] = q * OB + p
            return inner

        count = lax.div(q, z.group_size) + 1
        lax.fori_loop(0, count, block, 0)
        return b + count

    lax.fori_loop(0, z.degrees, degree, 0)


def pack(z, place, grid_field, f, slots, with_holder):
    total = z.devices * slots
    out_specs = [pl.BlockSpec((total, z.local, z.width), lambda i, *s: (0, 0, 0))]
    out_shape = [jax.ShapeDtypeStruct((total, z.local, z.width), jnp.bfloat16)]
    if with_holder:
        out_specs.append(pl.BlockSpec(memory_space=pltpu.SMEM))
        out_shape.append(jax.ShapeDtypeStruct((z.devices * z.capacity,), jnp.int32))
    return pl.pallas_call(
        functools.partial(pack_kernel, z),
        grid_spec=pltpu.PrefetchScalarGridSpec(
            num_scalar_prefetch=1,
            grid=(1,),
            in_specs=[
                pl.BlockSpec((1, z.local, z.blocks, z.width), lambda i, *s: (f, 0, 0, 0))
            ],
            out_specs=out_specs,
            scratch_shapes=[pltpu.VMEM((z.local * (z.blocks + 1), z.width), jnp.float32)],
        ),
        out_shape=out_shape,
        compiler_params=pltpu.CompilerParams(vmem_limit_bytes=48 << 20),
        cost_estimate=pl.CostEstimate(flops=10**9, bytes_accessed=10**7, transcendentals=0),
        name=f"pack_{f}",
    )(place, grid_field)


def solve_kernel(z, f, slots, per_step, holder_ref, start_ref, me_ref, columns_ref, inverses_ref, *rest):
    (own, across, along, corner, own_odd, across_odd, along_odd, corner_odd) = rest[:8]
    out_ref, matrix_ref, square_ref, above_ref, below_ref, sems = rest[8:]
    strength = diffusion_numbers[f]
    step = pl.program_id(0)
    shape = (z.levels, z.width)
    me = me_ref[0]

    @pl.when(step == 0)
    def _():
        sources = [
            own.at[f], own_odd.at[f], across.at[f], across_odd.at[f],
            along.at[f], along_odd.at[f], corner.at[0], corner_odd.at[0],
            inverses_ref.at[f, 0],
        ]
        copies = [
            pltpu.make_async_copy(source, matrix_ref.at[i], sems.at[i])
            for i, source in enumerate(sources)
        ]
        for copy in copies:
            copy.start()
        level = lax.broadcasted_iota(jnp.int32, shape, 0)

        def radius(positions):
            return inner_radius + shell_depth * (positions + 1).astype(jnp.float32) / (z.levels + 1)

        here = radius(level)
        scaled = (shell_depth / (z.levels + 1)) / here
        square_ref[...] = strength * (scaled * scaled)
        above_ref[...] = jnp.where(level == z.levels - 1, 0.0, strength * radius(level + 1) / here)
        below_ref[...] = jnp.where(level == 0, 0.0, strength * radius(level - 1) / here)
        for copy in copies:
            copy.wait()

    column = lax.broadcasted_iota(jnp.int32, shape, 1)
    for k in range(per_step):
        slot = jnp.minimum(step * per_step + k, slots - 1)
        code = holder_ref[me * slots + slot]
        q = lax.div(code, OB)
        value = z.spacing * (q + 1) - 1
        rank = lax.rem(lax.div(start_ref[q], z.capacity), PLANE)
        which = jnp.where(q >= z.degrees // 2, rank ^ lax.rem(me, PLANE), PLANE)
        factor = (value * (value + 1)).astype(jnp.float32)
        limit = 2 * (value - lax.rem(code, OB) * (z.width // 2)) + 1
        u = columns_ref[:, k].reshape(shape).astype(jnp.float32)
        u = jnp.where(column <= limit, u, 0.0)
        weight = (1.0 - 2.0 * strength) - factor * square_ref[...]
        rhs = weight * u
        rhs += above_ref[...] * pltpu.roll(u, z.levels - 1, 0)
        rhs += below_ref[...] * pltpu.roll(u, 1, 0)
        high = rhs.astype(jnp.bfloat16)
        low = (rhs - high.astype(jnp.float32)).astype(jnp.bfloat16)
        both = jnp.concatenate([high, low], axis=1)
        product = jnp.dot(matrix_ref[which], both, preferred_element_type=jnp.float32)
        solved = product[:, : z.width] + product[:, z.width :]
        out_ref[:, k] = solved.astype(jnp.bfloat16).reshape(z.devices, z.local, z.width)


def solve(z, holder, degree_start, me, columns, inverses, pieces, f, slots):
    steps = pl.cdiv(slots, 5)
    per_step = pl.cdiv(slots, steps)
    block = (z.devices, per_step, z.local, z.width)
    spec = pl.BlockSpec(block, lambda i, *s: (0, i, 0, 0))
    chosen = [part for side in pieces for part in (*side[:3], side[3 + f])]
    return pl.pallas_call(
        functools.partial(solve_kernel, z, f, slots, per_step),
        grid_spec=pltpu.PrefetchScalarGridSpec(
            num_scalar_prefetch=3,
            grid=(steps,),
            in_specs=[spec] + [pl.BlockSpec(memory_space=pl.ANY)] * (1 + len(chosen)),
            out_specs=spec,
            scratch_shapes=[pltpu.VMEM((PLANE + 1, z.levels, z.levels), jnp.bfloat16)]
            + [pltpu.VMEM((z.levels, z.width), jnp.float32)] * 3
            + [pltpu.SemaphoreType.DMA((PLANE + 1,))],
        ),
        out_shape=jax.ShapeDtypeStruct(columns.shape, jnp.bfloat16),
        compiler_params=pltpu.CompilerParams(vmem_limit_bytes=48 << 20),
        cost_estimate=pl.CostEstimate(flops=10**10, bytes_accessed=10**7, transcendentals=0),
        name=f"solve_{f}",
    )(holder, degree_start, me, columns, inverses, *chosen)


def unpack_kernel(z, place_ref, returned_ref, *rest):
    grid_ref, slope_ref, first_ref, last_ref, wide_ref = rest[-5:]
    pitch = z.blocks + 1

    def gather(g, carry):
        for k in range(GROUP):
            b = g * GROUP + k
            tile = returned_ref[place_ref[b]].astype(jnp.float32)
            wide_ref[pl.ds(b, z.local, stride=pitch), :] = tile
        return carry

    lax.fori_loop(0, z.blocks // GROUP, gather, 0)

    def group(g, carry):
        at = pl.multiple_of(g * GROUP, GROUP)
        rows = pl.ds(at, GROUP)
        value = [wide_ref[pl.ds(at + i * pitch, GROUP), :] for i in range(z.local)]
        for i in range(z.local):
            grid_ref[0, i, rows, :] = value[i].astype(jnp.bfloat16)
        for i in range(1, z.local - 1):
            slope = 0.5 * (value[i + 1] - value[i - 1])
            slope_ref[0, i, rows, :] = slope.astype(jnp.bfloat16)
        first_ref[0, rows, :] = value[0].astype(jnp.bfloat16)
        last_ref[0, rows, :] = value[-1].astype(jnp.bfloat16)
        return carry

    lax.fori_loop(0, z.blocks // GROUP, group, 0, unroll=2)


def unpack(z, place, returned, f, earlier):
    whole = jax.ShapeDtypeStruct((z.fields, z.local, z.blocks, z.width), jnp.bfloat16)
    level = jax.ShapeDtypeStruct((1, z.blocks, z.width), jnp.bfloat16)
    spec = pl.BlockSpec((1, z.local, z.blocks, z.width), lambda i, *s: (f, 0, 0, 0))
    level_spec = pl.BlockSpec(level.shape, lambda i, *s: (0, 0, 0))
    return pl.pallas_call(
        functools.partial(unpack_kernel, z),
        grid_spec=pltpu.PrefetchScalarGridSpec(
            num_scalar_prefetch=1,
            grid=(1,),
            in_specs=[pl.BlockSpec(returned.shape, lambda i, *s: (0, 0, 0))]
            + [pl.BlockSpec(memory_space=pl.ANY)] * len(earlier),
            out_specs=[spec, spec, level_spec, level_spec],
            scratch_shapes=[pltpu.VMEM((z.local * (z.blocks + 1), z.width), jnp.float32)],
        ),
        out_shape=[whole, whole, level, level],
        input_output_aliases={2 + i: i for i in range(len(earlier))},
        compiler_params=pltpu.CompilerParams(vmem_limit_bytes=48 << 20),
        cost_estimate=pl.CostEstimate(flops=10**9, bytes_accessed=10**7, transcendentals=0),
        name=f"unpack_{f}",
    )(place, returned, *earlier)


def edge_kernel(z, f, second_ref, before_last_ref, before_ref, after_ref, slope_in_ref, slope_ref,
                edge_ref, sems):
    del slope_in_ref

    def wide(ref):
        return ref[...].reshape(z.blocks, z.width).astype(jnp.float32)

    slopes = [wide(second_ref) - wide(before_ref), wide(after_ref) - wide(before_last_ref)]
    copies = []
    for i, level in enumerate((0, z.local - 1)):
        edge_ref[i] = (0.5 * slopes[i]).astype(jnp.bfloat16)
        copies.append(pltpu.make_async_copy(edge_ref.at[i], slope_ref.at[f, level], sems.at[i]))
        copies[i].start()
    for copy in copies:
        copy.wait()


def edges(z, slope, grid, before, after, f):
    block = (1, 1, z.blocks, z.width)
    beside_spec = pl.BlockSpec((1, z.blocks, z.width), lambda i: (0, 0, 0))
    return pl.pallas_call(
        functools.partial(edge_kernel, z, f),
        grid=(1,),
        in_specs=[
            pl.BlockSpec(block, lambda i: (f, 1, 0, 0)),
            pl.BlockSpec(block, lambda i: (f, z.local - 2, 0, 0)),
            beside_spec,
            beside_spec,
            pl.BlockSpec(memory_space=pl.ANY),
        ],
        out_specs=pl.BlockSpec(memory_space=pl.ANY),
        out_shape=jax.ShapeDtypeStruct(slope.shape, slope.dtype),
        scratch_shapes=[
            pltpu.VMEM((2, z.blocks, z.width), jnp.bfloat16),
            pltpu.SemaphoreType.DMA((2,)),
        ],
        input_output_aliases={4: 0},
        name=f"edges_{f}",
    )(grid, grid, before, after, slope)


def beside(z, first, last):
    up = [(i, i + 1) for i in range(z.devices - 1)]
    down = [(j, i) for i, j in up]
    return lax.ppermute(last, AXES, up), lax.ppermute(first, AXES, down)


def exchange(z, value, slots):
    shaped = value.reshape(z.devices, slots, z.local, z.width)
    return lax.all_to_all(shaped, AXES, split_axis=0, concat_axis=0, tiled=True)


def body(grid_field, inverses, slot_blocks, degree_start):
    rad, lm = lax.axis_size("rad"), lax.axis_size("lm")
    z = Sizes(rad * lm, grid_field, inverses, slot_blocks)
    choices = slot_choices(z)
    kernels = z.local % 16 == 0 and z.blocks % GROUP == 0 and rad % 2 == 0 and lm == PLANE // 2
    if not kernels or z.counts[z.degrees // 2 - 1] > choices[0]:
        return plain_body(z, grid_field, inverses, degree_start)
    me = lax.axis_index(AXES).reshape(1).astype(jnp.int32)
    choice, place = plan(z, degree_start, choices)
    routes = [functools.partial(route, z, slots) for slots in choices]
    return lax.switch(choice[0], routes, grid_field, inverses, degree_start, me, place)


def route(z, slots, grid_field, inverses, degree_start, me, place):
    (sent_0,) = pack(z, place, grid_field, 0, slots, False)
    sent_1, holder = pack(z, place, grid_field, 1, slots, True)
    straight = lax.optimization_barrier((sent_1, *straight_inverses(inverses)))
    columns = [exchange(z, sent, slots) for sent in (sent_0, straight[0])]
    pieces = lax.optimization_barrier(plane_inverses(*straight[1:]))
    solved = [
        solve(z, holder, degree_start, me, columns[f], inverses, pieces, f, slots)
        for f in range(z.fields)
    ]
    returned = [
        exchange(z, solved[f], slots).reshape(z.devices * slots, z.local, z.width)
        for f in range(z.fields)
    ]
    outs = ()
    for f in range(z.fields):
        grid, slope, first, last = unpack(z, place, returned[f], f, outs)
        outs = (grid, edges(z, slope, grid, *beside(z, first, last), f))
    return outs


def plain_body(z, grid_field, inverses, degree_start):
    index = np.arange(z.degrees)
    counts = np.asarray(z.counts)
    degree_of = np.repeat(index, counts)
    place_in = np.arange(z.blocks) - np.asarray(z.starts)[degree_of]
    value = z.spacing * (index + 1) - 1
    slot_place = degree_start[degree_of] + jnp.asarray(place_in, jnp.int32)
    total = z.devices * z.capacity
    holder = jnp.full((total,), z.blocks, jnp.int32)
    holder = holder.at[slot_place].set(jnp.arange(z.blocks, dtype=jnp.int32))
    sent = jnp.take(grid_field, holder, axis=2, mode="fill", fill_value=0)
    sent = sent.reshape(z.fields, z.local, z.devices, z.capacity, z.width)
    columns = lax.all_to_all(sent, AXES, split_axis=2, concat_axis=1, tiled=True)
    columns = columns.reshape(z.fields, z.levels, z.capacity, z.width)
    device = lax.axis_index(AXES)
    mine = lax.dynamic_slice_in_dim(holder, device * z.capacity, z.capacity)
    order = jnp.asarray(place_in)[:, None] * OB + np.arange(z.width)[None, :] // 2
    live_table = (order <= jnp.asarray(value[degree_of])[:, None]).astype(jnp.float32)
    live = jnp.take(live_table, mine, axis=0, mode="fill", fill_value=0)
    factor = (value * (value + 1)).astype(np.float32)[degree_of]
    factor = jnp.take(jnp.asarray(factor), mine, mode="fill", fill_value=0)
    upper = jnp.take(jnp.asarray(degree_of >= z.degrees // 2), mine, mode="fill", fill_value=False)
    radius = inner_radius + shell_depth * jnp.arange(z.levels + 2, dtype=jnp.float32) / (z.levels + 1)
    here = radius[1:-1][None, :, None, None]
    padded = jnp.pad(columns.astype(jnp.float32), ((0, 0), (1, 1), (0, 0), (0, 0)))
    weighted = padded * radius[None, :, None, None]
    second = (weighted[:, 2:] - 2.0 * weighted[:, 1:-1] + weighted[:, :-2]) / here
    scaled = (shell_depth / (z.levels + 1)) / here
    centre = padded[:, 1:-1]
    strength = jnp.asarray(diffusion_numbers, jnp.float32)[:, None, None, None]
    angular = factor[None, None, :, None] * (scaled * scaled) * centre
    rhs = (centre + strength * (second - angular)) * live[None, None]

    def solve_slot(carry, at):
        matrix = lax.dynamic_index_in_dim(
            inverses, upper[at].astype(jnp.int32), 1, keepdims=False
        ).astype(jnp.float32)
        block = lax.dynamic_index_in_dim(rhs, at, 2, keepdims=False)
        product = jnp.einsum("fij,fjc->fic", matrix, block, precision=lax.Precision.HIGHEST)
        return carry, product.astype(jnp.bfloat16)

    solved = lax.scan(solve_slot, 0, jnp.arange(z.capacity))[1]
    solved = jnp.moveaxis(solved, 0, 2)
    solved = solved.reshape(z.fields, z.devices, z.local, z.capacity, z.width)
    returned = lax.all_to_all(solved, AXES, split_axis=1, concat_axis=3, tiled=True)
    returned = returned.reshape(z.fields, z.local, total, z.width)
    grid = jnp.take(returned, slot_place, axis=2)
    before, after = beside(z, grid[:, :1], grid[:, -1:])
    rimmed = jnp.concatenate([before, grid, after], axis=1).astype(jnp.float32)
    return grid, (0.5 * (rimmed[:, 2:] - rimmed[:, :-2])).astype(jnp.bfloat16)


def solution(mesh):
    in_specs = (P(None, AXES), P(None, AXES), P(), P())
    out_specs = (P(None, AXES), P(None, AXES))
    return jax.shard_map(body, mesh=mesh, in_specs=in_specs, out_specs=out_specs, check_vma=False)
```

profile of v0, /device:TPU:15, one launch (start us, length us, event | category | flops | bytes accessed | tf_op | source)
XLA Modules:
  0.0 280.8 jit_solution(11849993130484525735)
XLA Ops:
  0.6 2.6 plan.1
  3.9 276.7 %conditional.1 = (bf16[2,16,544,128]{3,2,1,0:T(8,128)(2,1)}, bf16[2,16,544,128]{3,2,1,0:T(8,128)(2,1)}) conditional(s32[]{:T(128)} %bitcast.30, (s32[544]{0:T(1024)S(1)}, bf16[2,16,544,128]{3,2,1,0:T(8,128)(2,1)}, bf16[2,2,512,512]{3,2,1,0:T(8,128)(2,1)}, s32[64]{0:T(128)}, s32[]{:T(128)}, /*index=5*/s32[]{:T(128)}, ...), branch_computations={%region_0.0_spmd, %region_1.0_spmd, %region_2.0_spmd, %region_3.0_... | conditional | flops 24000000000 | bytes 194481968 | solution.py:378
  3.9 4.7 %pack_0.6 = bf16[608,16,128]{2,1,0:T(8,128)(2,1)} custom-call(s32[544]{0:T(1024)S(1)} %get-tuple-element.79.place_ref, bf16[2,16,544,128]{3,2,1,0:T(8,128)(2,1)} %get-tuple-element.218.field_ref), custom_call_target="tpu_custom_call" | custom-call | flops 1000000000 | bytes 10000000 | tf_op jit(solution)/shard_map/cond/branch_1_fun/pack_0/pallas_call | solution.py:164
  8.6 6.3 %all-to-all-start.6 = ((bf16[32,19,16,128]{3,2,1,0:T(8,128)(2,1)}), bf16[32,19,16,128]{3,2,1,0:T(8,128)(2,1)}, u32[]{:S(2)}, u32[]{:S(2)}) async-start(bf16[32,19,16,128]{3,2,1,0:T(8,128)(2,1)} %bitcast.10), calls=%async_computation.6 | async-start | bytes 4980736 | tf_op jit(solution)/shard_map/cond/branch_1_fun/all_to_all | solution.py:365
  14.9 0.1 slice_bitcast_fusion.1.rest_0_
  15.0 0.3 collective-permute-start.14
  15.4 0.3 collective-permute-start.13
  15.7 9.7 %pack_1.6 = (bf16[608,16,128]{2,1,0:T(8,128)(2,1)}, s32[768]{0:T(1024)S(1)}) custom-call(s32[544]{0:T(1024)S(1)} %get-tuple-element.79.place_ref, bf16[2,16,544,128]{3,2,1,0:T(8,128)(2,1)} %get-tuple-element.218.field_ref), custom_call_target="tpu_custom_call" | custom-call | flops 1000000000 | bytes 10000000 | tf_op jit(solution)/shard_map/cond/branch_1_fun/pack_1/pallas_call | solution.py:164
  25.4 39.4 %collective-permute-done.14.rest_2_ = bf16[2,512,512]{2,1,0:T(8,128)(2,1)S(1)} collective-permute-done((bf16[2,512,512]{2,1,0:T(8,128)(2,1)S(1)}, bf16[2,512,512]{2,1,0:T(8,128)(2,1)S(1)}, u32[]{:S(2)}, u32[]{:S(2)}) %collective-permute-start.14) | collective-permute-done | bytes 1048608 | tf_op jit(solution)/shard_map/cond/branch_1_fun/ppermute | solution.py:107
  64.8 0.0 collective-permute-done.13.rest_1_
  64.8 4.8 %all-to-all-done.6.columns_ref = bf16[32,19,16,128]{3,2,1,0:T(8,128)(2,1)} async-done(((bf16[32,19,16,128]{3,2,1,0:T(8,128)(2,1)}), bf16[32,19,16,128]{3,2,1,0:T(8,128)(2,1)}, u32[]{:S(2)}, u32[]{:S(2)}) %all-to-all-start.6) | async-done | bytes 2490400 | tf_op jit(solution)/shard_map/cond/branch_1_fun/all_to_all | solution.py:365
  69.5 6.9 %all-to-all-start.4 = ((bf16[32,19,16,128]{3,2,1,0:T(8,128)(2,1)}), bf16[32,19,16,128]{3,2,1,0:T(8,128)(2,1)}, u32[]{:S(2)}, u32[]{:S(2)}) async-start(bf16[32,19,16,128]{3,2,1,0:T(8,128)(2,1)} %bitcast.8), calls=%async_computation.4 | async-start | bytes 4980736 | tf_op jit(solution)/shard_map/cond/branch_1_fun/all_to_all | solution.py:365
  76.5 0.3 collective-permute-start.16
  76.9 0.3 collective-permute-start.15
  77.2 0.9 collective-permute-start.17
  78.1 0.0 collective-permute-start.18
  78.1 0.5 collective-permute-start.19
  78.7 31.0 %collective-permute-done.16.rest_3_ = bf16[1,512,512]{2,1,0:T(8,128)(2,1)} collective-permute-done((bf16[1,512,512]{2,1,0:T(8,128)(2,1)S(1)}, bf16[1,512,512]{2,1,0:T(8,128)(2,1)}, u32[]{:S(2)}, u32[]{:S(2)}) %collective-permute-start.16) | collective-permute-done | bytes 524320 | tf_op jit(solution)/shard_map/cond/branch_1_fun/ppermute | solution.py:107
  109.7 1.3 collective-permute-start.21
  111.0 0.0 collective-permute-done.15.rest_3_
  111.0 0.0 collective-permute-start.20
  111.0 1.9 collective-permute-done.21.rest_7_
  112.9 0.7 collective-permute-done.20.rest_7_
  113.7 9.1 %solve_0.6 = bf16[32,19,16,128]{3,2,1,0:T(8,128)(2,1)} custom-call(s32[768]{0:T(1024)S(1)} %get-tuple-element.81.holder_ref, s32[64]{0:T(128)S(1)} %copy-done.62, s32[1]{0:T(128)} %bitcast.6.me_ref, bf16[32,19,16,128]{3,2,1,0:T(8,128)(2,1)} %all-to-all-done.6.columns_ref, bf16[2,2,512,512]{3,2,1,0:T(8,128)(2,1)} %get-tuple-element.256.inverses_ref, ...), custom_call_target="tpu_custom_call" | custom-call | flops 10000000000 | bytes 10000000 | tf_op jit(solution)/shard_map/cond/branch_1_fun/solve_0/pallas_call | solution.py:246
  122.8 8.2 %all-to-all-done.4.columns_ref = bf16[32,19,16,128]{3,2,1,0:T(8,128)(2,1)} async-done(((bf16[32,19,16,128]{3,2,1,0:T(8,128)(2,1)}), bf16[32,19,16,128]{3,2,1,0:T(8,128)(2,1)}, u32[]{:S(2)}, u32[]{:S(2)}) %all-to-all-start.4) | async-done | bytes 2490400 | tf_op jit(solution)/shard_map/cond/branch_1_fun/all_to_all | solution.py:365
  131.0 6.8 %all-to-all-start.7 = ((bf16[32,19,16,128]{3,2,1,0:T(8,128)(2,1)}), bf16[32,19,16,128]{3,2,1,0:T(8,128)(2,1)S(1)}, u32[]{:S(2)}, u32[]{:S(2)}) async-start(bf16[32,19,16,128]{3,2,1,0:T(8,128)(2,1)} %solve_0.6), calls=%async_computation.7 | async-start | bytes 4980736 | tf_op jit(solution)/shard_map/cond/branch_1_fun/all_to_all | solution.py:365
  137.9 1.2 copy-done.19
  139.1 1.2 copy-done.29
  140.3 9.1 %solve_1.6 = bf16[32,19,16,128]{3,2,1,0:T(8,128)(2,1)} custom-call(s32[768]{0:T(1024)S(1)} %get-tuple-element.81.holder_ref, s32[64]{0:T(128)S(1)} %copy-done.62, s32[1]{0:T(128)} %bitcast.6.me_ref, bf16[32,19,16,128]{3,2,1,0:T(8,128)(2,1)} %all-to-all-done.4.columns_ref, bf16[2,2,512,512]{3,2,1,0:T(8,128)(2,1)} %get-tuple-element.256.inverses_ref, ...), custom_call_target="tpu_custom_call" | custom-call | flops 10000000000 | bytes 10000000 | tf_op jit(solution)/shard_map/cond/branch_1_fun/solve_1/pallas_call | solution.py:246
  149.5 43.0 %all-to-all-done.7 = bf16[32,19,16,128]{3,2,1,0:T(8,128)(2,1)S(1)} async-done(((bf16[32,19,16,128]{3,2,1,0:T(8,128)(2,1)}), bf16[32,19,16,128]{3,2,1,0:T(8,128)(2,1)S(1)}, u32[]{:S(2)}, u32[]{:S(2)}) %all-to-all-start.7) | async-done | bytes 2490400 | tf_op jit(solution)/shard_map/cond/branch_1_fun/all_to_all | solution.py:365
  192.5 1.4 copy-done.6
  193.9 6.7 %all-to-all-start.5 = ((bf16[32,19,16,128]{3,2,1,0:T(8,128)(2,1)}), bf16[32,19,16,128]{3,2,1,0:T(8,128)(2,1)S(1)}, u32[]{:S(2)}, u32[]{:S(2)}) async-start(bf16[32,19,16,128]{3,2,1,0:T(8,128)(2,1)} %solve_1.6), calls=%async_computation.5 | async-start | bytes 4980736 | tf_op jit(solution)/shard_map/cond/branch_1_fun/all_to_all | solution.py:365
  200.7 0.0 copy-start.7
  200.7 1.7 copy-done.7
  202.4 4.0 %unpack_0.6 = (bf16[2,16,544,128]{3,2,1,0:T(8,128)(2,1)}, bf16[2,16,544,128]{3,2,1,0:T(8,128)(2,1)}, bf16[1,544,128]{2,1,0:T(8,128)(2,1)S(1)}, bf16[1,544,128]{2,1,0:T(8,128)(2,1)S(1)}) custom-call(s32[544]{0:T(1024)S(1)} %get-tuple-element.79.place_ref, bf16[608,16,128]{2,1,0:T(8,128)(2,1)S(1)} %bitcast.44), custom_call_target="tpu_custom_call" | custom-call | flops 1000000000 | bytes 10000000 | tf_op jit(solution)/shard_map/cond/branch_1_fun/unpack_0/pallas_call | solution.py:298
  206.3 3.3 %collective-permute-start.22 = (bf16[1,544,128]{2,1,0:T(8,128)(2,1)S(1)}, bf16[1,544,128]{2,1,0:T(8,128)(2,1)S(1)}, u32[]{:S(2)}, u32[]{:S(2)}) collective-permute-start(bf16[1,544,128]{2,1,0:T(8,128)(2,1)S(1)} %get-tuple-element.101), channel_id=1, source_target_pairs={{0,1},{1,2},{2,3},{3,4},{4,5},{5,6},{6,7},{7,8},{8,9},{9,10},{10,1... | collective-permute-start | bytes 417800 | tf_op jit(solution)/shard_map/cond/branch_1_fun/ppermute | solution.py:360
  209.7 1.9 collective-permute-start.23
  211.6 45.1 %collective-permute-done.22.before_ref = bf16[1,544,128]{2,1,0:T(8,128)(2,1)S(1)} collective-permute-done((bf16[1,544,128]{2,1,0:T(8,128)(2,1)S(1)}, bf16[1,544,128]{2,1,0:T(8,128)(2,1)S(1)}, u32[]{:S(2)}, u32[]{:S(2)}) %collective-permute-start.22) | collective-permute-done | bytes 139296 | tf_op jit(solution)/shard_map/cond/branch_1_fun/ppermute | solution.py:360
  256.7 1.3 collective-permute-done.23.after_ref
  258.0 0.6 copy-done.53
  258.7 1.9 edges_0.6.rest_1_
  260.6 4.0 %unpack_1.6 = (bf16[2,16,544,128]{3,2,1,0:T(8,128)(2,1)}, bf16[2,16,544,128]{3,2,1,0:T(8,128)(2,1)}, bf16[1,544,128]{2,1,0:T(8,128)(2,1)S(1)}, bf16[1,544,128]{2,1,0:T(8,128)(2,1)S(1)}) custom-call(s32[544]{0:T(1024)S(1)} %get-tuple-element.79.place_ref, bf16[608,16,128]{2,1,0:T(8,128)(2,1)S(1)} %bitcast.39, ...), custom_call_target="tpu_custom_call", output_to_operand_aliasing={{0}: (2, {}), {1}: (3, {})} | custom-call | flops 1000000000 | bytes 10000000 | tf_op jit(solution)/shard_map/cond/branch_1_fun/unpack_1/pallas_call | solution.py:298
  264.5 5.0 %collective-permute-start.24 = (bf16[1,544,128]{2,1,0:T(8,128)(2,1)S(1)}, bf16[1,544,128]{2,1,0:T(8,128)(2,1)S(1)}, u32[]{:S(2)}, u32[]{:S(2)}) collective-permute-start(bf16[1,544,128]{2,1,0:T(8,128)(2,1)S(1)} %get-tuple-element.105), channel_id=1, source_target_pairs={{0,1},{1,2},{2,3},{3,4},{4,5},{5,6},{6,7},{7,8},{8,9},{9,10},{10,1... | collective-permute-start | bytes 417800 | tf_op jit(solution)/shard_map/cond/branch_1_fun/ppermute | solution.py:360
  269.5 1.9 collective-permute-start.25
  271.4 0.1 collective-permute-done.24.before_ref
  271.5 6.2 %collective-permute-done.25.after_ref = bf16[1,544,128]{2,1,0:T(8,128)(2,1)S(1)} collective-permute-done((bf16[1,544,128]{2,1,0:T(8,128)(2,1)S(1)}, bf16[1,544,128]{2,1,0:T(8,128)(2,1)S(1)}, u32[]{:S(2)}, u32[]{:S(2)}) %collective-permute-start.25) | collective-permute-done | bytes 139296 | tf_op jit(solution)/shard_map/cond/branch_1_fun/ppermute | solution.py:360
  277.7 0.6 copy-done.54
  278.3 1.9 edges_1.6
  (23 shorter events, 0.1 us)
Async XLA Ops:
  8.6 6.3 %copy-start.37 = (bf16[2,2,512,512]{3,2,1,0:T(8,128)(2,1)S(1)}, bf16[2,2,512,512]{3,2,1,0:T(8,128)(2,1)}, u32[]{:S(2)}) copy-start(bf16[2,2,512,512]{3,2,1,0:T(8,128)(2,1)} %get-tuple-element.256.inverses_ref) | copy-start | bytes 6291460 | tf_op jit(solution)/shard_map/cond
  8.6 60.9 %all-to-all-start.6 = ((bf16[32,19,16,128]{3,2,1,0:T(8,128)(2,1)}), bf16[32,19,16,128]{3,2,1,0:T(8,128)(2,1)}, u32[]{:S(2)}, u32[]{:S(2)}) async-start(bf16[32,19,16,128]{3,2,1,0:T(8,128)(2,1)} %bitcast.10), calls=%async_computation.6 | async-start | bytes 4980736 | tf_op jit(solution)/shard_map/cond/branch_1_fun/all_to_all | solution.py:365
  15.0 49.8 %collective-permute-start.14 = (bf16[2,512,512]{2,1,0:T(8,128)(2,1)S(1)}, bf16[2,512,512]{2,1,0:T(8,128)(2,1)S(1)}, u32[]{:S(2)}, u32[]{:S(2)}) collective-permute-start(bf16[2,512,512]{2,1,0:T(8,128)(2,1)S(1)} %slice_bitcast_fusion.1.rest_0_), channel_id=1, source_target_pairs={{0,4},{4,0},{8,12},{12,8},{16,20},{20,16},{24,28},{28,24},{1,5},{5... | collective-permute-start | bytes 3145736 | tf_op jit(solution)/shard_map/cond/branch_1_fun/ppermute | solution.py:107
  15.4 49.4 %collective-permute-start.13 = (bf16[2,512,512]{2,1,0:T(8,128)(2,1)S(1)}, bf16[2,512,512]{2,1,0:T(8,128)(2,1)S(1)}, u32[]{:S(2)}, u32[]{:S(2)}) collective-permute-start(bf16[2,512,512]{2,1,0:T(8,128)(2,1)S(1)} %slice_bitcast_fusion.1.rest_0_), channel_id=1, source_target_pairs={{0,2},{1,3},{2,0},{3,1},{4,6},{5,7},{6,4},{7,5},{8,10},{9,11},{10,... | collective-permute-start | bytes 3145736 | tf_op jit(solution)/shard_map/cond/branch_1_fun/ppermute | solution.py:107
  64.8 48.9 %copy-start.18 = (bf16[2,512,512]{2,1,0:T(8,128)(2,1)}, bf16[2,512,512]{2,1,0:T(8,128)(2,1)S(1)}, u32[]{:S(2)}) copy-start(bf16[2,512,512]{2,1,0:T(8,128)(2,1)S(1)} %collective-permute-done.14.rest_2_) | copy-start | bytes 3145732 | tf_op jit(solution)/shard_map/cond
  64.8 48.9 %copy-start.28 = (bf16[2,512,512]{2,1,0:T(8,128)(2,1)}, bf16[2,512,512]{2,1,0:T(8,128)(2,1)S(1)}, u32[]{:S(2)}) copy-start(bf16[2,512,512]{2,1,0:T(8,128)(2,1)S(1)} %collective-permute-done.13.rest_1_) | copy-start | bytes 3145732 | tf_op jit(solution)/shard_map/cond
  69.5 44.1 %copy-start.62 = (s32[64]{0:T(128)S(1)}, s32[64]{0:T(128)}, u32[]{:S(2)}) copy-start(s32[64]{0:T(128)} %get-tuple-element.82.start_ref) | copy-start | bytes 772 | tf_op jit(solution)/shard_map/cond
  69.5 61.5 %all-to-all-start.4 = ((bf16[32,19,16,128]{3,2,1,0:T(8,128)(2,1)}), bf16[32,19,16,128]{3,2,1,0:T(8,128)(2,1)}, u32[]{:S(2)}, u32[]{:S(2)}) async-start(bf16[32,19,16,128]{3,2,1,0:T(8,128)(2,1)} %bitcast.8), calls=%async_computation.4 | async-start | bytes 4980736 | tf_op jit(solution)/shard_map/cond/branch_1_fun/all_to_all | solution.py:365
  76.5 33.2 %collective-permute-start.16 = (bf16[1,512,512]{2,1,0:T(8,128)(2,1)S(1)}, bf16[1,512,512]{2,1,0:T(8,128)(2,1)}, u32[]{:S(2)}, u32[]{:S(2)}) collective-permute-start(bf16[1,512,512]{2,1,0:T(8,128)(2,1)S(1)} %slice.35), channel_id=1, source_target_pairs={{0,2},{1,3},{2,0},{3,1},{4,6},{5,7},{6,4},{7,5},{8,10},{9,11},{10,... | collective-permute-start | bytes 1572872 | tf_op jit(solution)/shard_map/cond/branch_1_fun/ppermute | solution.py:107
  76.9 34.2 %collective-permute-start.15 = (bf16[1,512,512]{2,1,0:T(8,128)(2,1)S(1)}, bf16[1,512,512]{2,1,0:T(8,128)(2,1)}, u32[]{:S(2)}, u32[]{:S(2)}) collective-permute-start(bf16[1,512,512]{2,1,0:T(8,128)(2,1)S(1)} %slice.34), channel_id=1, source_target_pairs={{0,4},{4,0},{8,12},{12,8},{16,20},{20,16},{24,28},{28,24},{1,5},{5... | collective-permute-start | bytes 1572872 | tf_op jit(solution)/shard_map/cond/branch_1_fun/ppermute | solution.py:107
  77.2 36.4 %collective-permute-start.17 = (bf16[2,512,512]{2,1,0:T(8,128)(2,1)S(1)}, bf16[2,512,512]{2,1,0:T(8,128)(2,1)}, u32[]{:S(2)}, u32[]{:S(2)}) collective-permute-start(bf16[2,512,512]{2,1,0:T(8,128)(2,1)S(1)} %slice_bitcast_fusion.1.rest_0_), channel_id=1, source_target_pairs={{0,1},{1,0},{2,3},{3,2},{4,5},{5,4},{6,7},{7,6},{8,9},{9,8},{10,11... | collective-permute-start | bytes 3145736 | tf_op jit(solution)/shard_map/cond/branch_1_fun/ppermute | solution.py:107
  78.1 35.5 %collective-permute-start.18 = (bf16[2,512,512]{2,1,0:T(8,128)(2,1)S(1)}, bf16[2,512,512]{2,1,0:T(8,128)(2,1)}, u32[]{:S(2)}, u32[]{:S(2)}) collective-permute-start(bf16[2,512,512]{2,1,0:T(8,128)(2,1)S(1)} %collective-permute-done.13.rest_1_), channel_id=1, source_target_pairs={{0,1},{1,0},{2,3},{3,2},{4,5},{5,4},{6,7},{7,6},{8,9},{9,8},{10,11... | collective-permute-start | bytes 3145736 | tf_op jit(solution)/shard_map/cond/branch_1_fun/ppermute | solution.py:107
  78.1 35.5 %collective-permute-start.19 = (bf16[2,512,512]{2,1,0:T(8,128)(2,1)S(1)}, bf16[2,512,512]{2,1,0:T(8,128)(2,1)}, u32[]{:S(2)}, u32[]{:S(2)}) collective-permute-start(bf16[2,512,512]{2,1,0:T(8,128)(2,1)S(1)} %collective-permute-done.14.rest_2_), channel_id=1, source_target_pairs={{0,1},{1,0},{2,3},{3,2},{4,5},{5,4},{6,7},{7,6},{8,9},{9,8},{10,11... | collective-permute-start | bytes 3145736 | tf_op jit(solution)/shard_map/cond/branch_1_fun/ppermute | solution.py:107
  109.7 3.2 %collective-permute-start.21 = (bf16[1,512,512]{2,1,0:T(8,128)(2,1)}, bf16[1,512,512]{2,1,0:T(8,128)(2,1)}, u32[]{:S(2)}, u32[]{:S(2)}) collective-permute-start(bf16[1,512,512]{2,1,0:T(8,128)(2,1)} %collective-permute-done.16.rest_3_), channel_id=1, source_target_pairs={{0,1},{1,0},{2,3},{3,2},{4,5},{5,4},{6,7},{7,6},{8,9},{9,8},{10,11... | collective-permute-start | bytes 1572872 | tf_op jit(solution)/shard_map/cond/branch_1_fun/ppermute | solution.py:107
  111.0 2.6 collective-permute-start.20
  131.0 61.5 %all-to-all-start.7 = ((bf16[32,19,16,128]{3,2,1,0:T(8,128)(2,1)}), bf16[32,19,16,128]{3,2,1,0:T(8,128)(2,1)S(1)}, u32[]{:S(2)}, u32[]{:S(2)}) async-start(bf16[32,19,16,128]{3,2,1,0:T(8,128)(2,1)} %solve_0.6), calls=%async_computation.7 | async-start | bytes 4980736 | tf_op jit(solution)/shard_map/cond/branch_1_fun/all_to_all | solution.py:365
  137.9 1.2 copy-start.19
  139.1 1.2 copy-start.29
  192.5 1.4 copy-start.6
  193.9 66.6 %all-to-all-start.5 = ((bf16[32,19,16,128]{3,2,1,0:T(8,128)(2,1)}), bf16[32,19,16,128]{3,2,1,0:T(8,128)(2,1)S(1)}, u32[]{:S(2)}, u32[]{:S(2)}) async-start(bf16[32,19,16,128]{3,2,1,0:T(8,128)(2,1)} %solve_1.6), calls=%async_computation.5 | async-start | bytes 4980736 | tf_op jit(solution)/shard_map/cond/branch_1_fun/all_to_all | solution.py:365
  200.7 1.7 copy-start.7
  206.3 50.4 %collective-permute-start.22 = (bf16[1,544,128]{2,1,0:T(8,128)(2,1)S(1)}, bf16[1,544,128]{2,1,0:T(8,128)(2,1)S(1)}, u32[]{:S(2)}, u32[]{:S(2)}) collective-permute-start(bf16[1,544,128]{2,1,0:T(8,128)(2,1)S(1)} %get-tuple-element.101), channel_id=1, source_target_pairs={{0,1},{1,2},{2,3},{3,4},{4,5},{5,6},{6,7},{7,8},{8,9},{9,10},{10,1... | collective-permute-start | bytes 417800 | tf_op jit(solution)/shard_map/cond/branch_1_fun/ppermute | solution.py:360
  209.7 48.3 %collective-permute-start.23 = (bf16[1,544,128]{2,1,0:T(8,128)(2,1)S(1)}, bf16[1,544,128]{2,1,0:T(8,128)(2,1)S(1)}, u32[]{:S(2)}, u32[]{:S(2)}) collective-permute-start(bf16[1,544,128]{2,1,0:T(8,128)(2,1)S(1)} %get-tuple-element.102), channel_id=1, source_target_pairs={{1,0},{2,1},{3,2},{4,3},{5,4},{6,5},{7,6},{8,7},{9,8},{10,9},{11,1... | collective-permute-start | bytes 417800 | tf_op jit(solution)/shard_map/cond/branch_1_fun/ppermute | solution.py:360
  256.7 1.3 copy-start.43
  258.0 0.7 copy-start.53
  264.5 7.0 %collective-permute-start.24 = (bf16[1,544,128]{2,1,0:T(8,128)(2,1)S(1)}, bf16[1,544,128]{2,1,0:T(8,128)(2,1)S(1)}, u32[]{:S(2)}, u32[]{:S(2)}) collective-permute-start(bf16[1,544,128]{2,1,0:T(8,128)(2,1)S(1)} %get-tuple-element.105), channel_id=1, source_target_pairs={{0,1},{1,2},{2,3},{3,4},{4,5},{5,6},{6,7},{7,8},{8,9},{9,10},{10,1... | collective-permute-start | bytes 417800 | tf_op jit(solution)/shard_map/cond/branch_1_fun/ppermute | solution.py:360
  269.5 8.2 %collective-permute-start.25 = (bf16[1,544,128]{2,1,0:T(8,128)(2,1)S(1)}, bf16[1,544,128]{2,1,0:T(8,128)(2,1)S(1)}, u32[]{:S(2)}, u32[]{:S(2)}) collective-permute-start(bf16[1,544,128]{2,1,0:T(8,128)(2,1)S(1)} %get-tuple-element.106), channel_id=1, source_target_pairs={{1,0},{2,1},{3,2},{4,3},{5,4},{6,5},{7,6},{8,7},{9,8},{10,9},{11,1... | collective-permute-start | bytes 417800 | tf_op jit(solution)/shard_map/cond/branch_1_fun/ppermute | solution.py:360
  271.5 6.2 %copy-start.44 = (bf16[1,544,128]{2,1,0:T(8,128)(2,1)}, bf16[1,544,128]{2,1,0:T(8,128)(2,1)S(1)}, u32[]{:S(2)}) copy-start(bf16[1,544,128]{2,1,0:T(8,128)(2,1)S(1)} %collective-permute-done.24.before_ref) | copy-start | bytes 417796 | tf_op jit(solution)/shard_map/cond
  277.7 0.7 copy-start.54
where the time goes:
time: 282 us; the launch traced here: 281 us
  waiting for transfers between devices  182 us (65%)
  Pallas kernels  46.9 us (17%)
  starting transfers between devices  43 us (15%)
  local copies, waits for them, and re-layouts  7.05 us (2%)
    ppermute x9, waiting for transfers between devices, swap(): return lax.ppermute(value, axis, [(i, i ^ bit) for i in range(size)])  73 us
    all_to_all x4, waiting for transfers between devices, exchange(): return lax.all_to_all(shaped, AXES, split_axis=0, concat_axis=0, tiled=True)  56 us
    ppermute x4, waiting for transfers between devices, beside(): return (lax.ppermute(last, AXES, up), lax.ppermute(first, AXES, down))  52.7 us
    all_to_all x4, starting transfers between devices, exchange(): return lax.all_to_all(shaped, AXES, split_axis=0, concat_axis=0, tiled=True)  26.8 us
    pallas_call x2, Pallas kernels, solve(): pl.pallas_call(functools.partial(solve_kernel, z, f, slots, per_step), gr...  18.2 us
    pallas_call x2, Pallas kernels, pack(): pl.pallas_call(functools.partial(pack_kernel, z), grid_spec=pltpu.Prefetc...  14.4 us
    ppermute x4, starting transfers between devices, beside(): return (lax.ppermute(last, AXES, up), lax.ppermute(first, AXES, down))  12.1 us
    pallas_call x2, Pallas kernels, unpack(): pl.pallas_call(functools.partial(unpack_kernel, z), grid_spec=pltpu.Prefe...  7.94 us
  transfers between devices with their start and end apart: 17, of which 11 were waited for; matrix products, arithmetic and copies ran while one was open for 0% of the time, Pallas kernels for 12%

commit v1 on v0

--- a/solution.py
+++ b/solution.py
@@ -12,7 +12,9 @@
 OB = 64
 AXES = ("rad", "lm")
 PLANE = 8
+GIFT = 8
 GROUP = 16
+VMEM = 48 << 20
 
 inner_radius = 0.35
 shell_depth = 0.65
@@ -35,24 +37,32 @@
 
 def slot_choices(z):
     mean = -(-z.blocks // z.devices)
-    return sorted({min(mean + extra, z.capacity) for extra in (1, 2, 3, 4)} | {z.capacity})
-
-
-def plan_kernel(z, choices, start_ref, choice_ref, place_ref, load_ref, device_ref, next_ref):
+    return sorted({min(mean + extra, z.capacity) for extra in (0, 1, 2, 3)} | {z.capacity})
+
+
+def plan_kernel(z, choices, start_ref, choice_ref, place_ref, load_ref, room_ref, device_ref, next_ref):
     half = z.degrees // 2
     planes = z.devices // PLANE
     owner = [lax.div(start_ref[q], z.capacity) for q in range(z.degrees)]
     for q in range(half, z.degrees):
         load_ref[owner[q]] = start_ref[q] - owner[q] * z.capacity + z.counts[q]
-    totals = [sum(load_ref[g * PLANE + e] for e in range(PLANE)) for g in range(planes)]
-    most = functools.reduce(jnp.maximum, totals)
+    loads = [load_ref[d] for d in range(z.devices)]
+    totals = [sum(loads[g * PLANE : (g + 1) * PLANE]) for g in range(planes)]
+    most = functools.reduce(jnp.maximum, [totals[g] + totals[g + 1] for g in range(0, planes, 2)])
     choice = jnp.int32(0)
     slots = jnp.int32(choices[0])
+    highest = functools.reduce(jnp.maximum, totals)
     for i in range(1, len(choices)):
-        beyond = most > PLANE * choices[i - 1]
+        tried = choices[i - 1]
+        beyond = (most > 2 * PLANE * tried) | (highest > PLANE * tried + GIFT * PLANE // 2)
         choice = jnp.where(beyond, i, choice)
         slots = jnp.where(beyond, choices[i], slots)
     choice_ref[0] = choice
+    for d in range(z.devices):
+        excess = totals[d // PLANE] - PLANE * slots - GIFT * (d % PLANE // 2)
+        gift = jnp.int32(0) if d % 2 else jnp.clip(excess, 0, GIFT)
+        load_ref[d] = loads[d] - gift
+        room_ref[d ^ PLANE] = slots - gift
     for g in range(planes):
         device_ref[g] = g * PLANE
         next_ref[g] = load_ref[g * PLANE]
@@ -61,14 +71,13 @@
         for p in range(z.counts[q]):
             place_ref[z.starts[q] + p] = first + p
     for q in range(half, z.degrees):
-        if z.counts[half - 1] + z.counts[q] <= choices[0]:
-            continue
         plane = lax.div(owner[q], PLANE)
-        room = slots - (start_ref[q] - owner[q] * z.capacity)
+        offset = start_ref[q] - owner[q] * z.capacity
+        kept = load_ref[owner[q]] - offset
 
         def move(p, carry, plane=plane, q=q):
             def full(state):
-                return state[1] >= slots
+                return state[1] >= room_ref[state[0]]
 
             def advance(state):
                 return state[0] + 1, load_ref[state[0] + 1]
@@ -79,7 +88,15 @@
             place_ref[z.starts[q] + p] = holder * slots + slot
             return carry
 
-        lax.fori_loop(jnp.minimum(room, z.counts[q]), z.counts[q], move, 0)
+        lax.fori_loop(jnp.minimum(room_ref[owner[q]] - offset, kept), kept, move, 0)
+        other = owner[q] ^ PLANE
+        given = other * slots + room_ref[other] - kept
+
+        def give(p, carry, given=given, q=q):
+            place_ref[z.starts[q] + p] = given + p
+            return carry
+
+        lax.fori_loop(kept, z.counts[q], give, 0)
 
 
 def plan(z, degree_start, choices):
@@ -95,6 +112,7 @@
         ],
         scratch_shapes=[
             pltpu.SMEM((z.devices,), jnp.int32),
+            pltpu.SMEM((z.devices,), jnp.int32),
             pltpu.SMEM((planes,), jnp.int32),
             pltpu.SMEM((planes,), jnp.int32),
         ],
@@ -109,13 +127,13 @@
 
 def straight_inverses(inverses):
     own = inverses[:, 1]
-    return own, swap(own, "lm", 2), swap(own, "rad", 1)
-
-
-def plane_inverses(own, across, along):
-    corner = [swap(across[:1], "rad", 1), swap(along[1:], "lm", 2)]
-    even = [own, across, along] + corner
-    return even, [swap(value, "lm", 1) for value in even]
+    rad, lm = lax.axis_size("rad"), lax.axis_size("lm")
+    facing = [(d, d ^ PLANE) for d in range(0, rad * lm, 2)]
+    return own, swap(own, "lm", 2), swap(own, "rad", 1), lax.ppermute(own, AXES, facing)
+
+
+def other_core(values):
+    return [swap(value, "lm", 1) for value in values]
 
 
 def pack_kernel(z, place_ref, field_ref, out_ref, *rest):
@@ -173,15 +191,15 @@
             scratch_shapes=[pltpu.VMEM((z.local * (z.blocks + 1), z.width), jnp.float32)],
         ),
         out_shape=out_shape,
-        compiler_params=pltpu.CompilerParams(vmem_limit_bytes=48 << 20),
+        compiler_params=pltpu.CompilerParams(vmem_limit_bytes=VMEM),
         cost_estimate=pl.CostEstimate(flops=10**9, bytes_accessed=10**7, transcendentals=0),
         name=f"pack_{f}",
     )(place, grid_field)
 
 
 def solve_kernel(z, f, slots, per_step, holder_ref, start_ref, me_ref, columns_ref, inverses_ref, *rest):
-    (own, across, along, corner, own_odd, across_odd, along_odd, corner_odd) = rest[:8]
-    out_ref, matrix_ref, square_ref, above_ref, below_ref, sems = rest[8:]
+    (own, across, along, corner, own_odd, across_odd, along_odd, corner_odd, far) = rest[:9]
+    out_ref, matrix_ref, square_ref, above_ref, below_ref, sems = rest[9:]
     strength = diffusion_numbers[f]
     step = pl.program_id(0)
     shape = (z.levels, z.width)
@@ -192,7 +210,7 @@
         sources = [
             own.at[f], own_odd.at[f], across.at[f], across_odd.at[f],
             along.at[f], along_odd.at[f], corner.at[0], corner_odd.at[0],
-            inverses_ref.at[f, 0],
+            inverses_ref.at[f, 0], far.at[f],
         ]
         copies = [
             pltpu.make_async_copy(source, matrix_ref.at[i], sems.at[i])
@@ -219,8 +237,9 @@
         code = holder_ref[me * slots + slot]
         q = lax.div(code, OB)
         value = z.spacing * (q + 1) - 1
-        rank = lax.rem(lax.div(start_ref[q], z.capacity), PLANE)
-        which = jnp.where(q >= z.degrees // 2, rank ^ lax.rem(me, PLANE), PLANE)
+        offset = lax.div(start_ref[q], z.capacity) ^ me
+        which = jnp.where(offset < PLANE, offset, PLANE + 1)
+        which = jnp.where(q >= z.degrees // 2, which, PLANE)
         factor = (value * (value + 1)).astype(jnp.float32)
         limit = 2 * (value - lax.rem(code, OB) * (z.width // 2)) + 1
         u = columns_ref[:, k].reshape(shape).astype(jnp.float32)
@@ -242,23 +261,22 @@
     per_step = pl.cdiv(slots, steps)
     block = (z.devices, per_step, z.local, z.width)
     spec = pl.BlockSpec(block, lambda i, *s: (0, i, 0, 0))
-    chosen = [part for side in pieces for part in (*side[:3], side[3 + f])]
     return pl.pallas_call(
         functools.partial(solve_kernel, z, f, slots, per_step),
         grid_spec=pltpu.PrefetchScalarGridSpec(
             num_scalar_prefetch=3,
             grid=(steps,),
-            in_specs=[spec] + [pl.BlockSpec(memory_space=pl.ANY)] * (1 + len(chosen)),
+            in_specs=[spec] + [pl.BlockSpec(memory_space=pl.ANY)] * (1 + len(pieces)),
             out_specs=spec,
-            scratch_shapes=[pltpu.VMEM((PLANE + 1, z.levels, z.levels), jnp.bfloat16)]
+            scratch_shapes=[pltpu.VMEM((PLANE + 2, z.levels, z.levels), jnp.bfloat16)]
             + [pltpu.VMEM((z.levels, z.width), jnp.float32)] * 3
-            + [pltpu.SemaphoreType.DMA((PLANE + 1,))],
+            + [pltpu.SemaphoreType.DMA((PLANE + 2,))],
         ),
         out_shape=jax.ShapeDtypeStruct(columns.shape, jnp.bfloat16),
-        compiler_params=pltpu.CompilerParams(vmem_limit_bytes=48 << 20),
+        compiler_params=pltpu.CompilerParams(vmem_limit_bytes=VMEM),
         cost_estimate=pl.CostEstimate(flops=10**10, bytes_accessed=10**7, transcendentals=0),
         name=f"solve_{f}",
-    )(holder, degree_start, me, columns, inverses, *chosen)
+    )(holder, degree_start, me, columns, inverses, *pieces)
 
 
 def unpack_kernel(z, place_ref, returned_ref, *rest):
@@ -307,7 +325,7 @@
         ),
         out_shape=[whole, whole, level, level],
         input_output_aliases={2 + i: i for i in range(len(earlier))},
-        compiler_params=pltpu.CompilerParams(vmem_limit_bytes=48 << 20),
+        compiler_params=pltpu.CompilerParams(vmem_limit_bytes=VMEM if earlier else 60 << 20),
         cost_estimate=pl.CostEstimate(flops=10**9, bytes_accessed=10**7, transcendentals=0),
         name=f"unpack_{f}",
     )(place, returned, *earlier)
@@ -350,6 +368,7 @@
             pltpu.SemaphoreType.DMA((2,)),
         ],
         input_output_aliases={4: 0},
+        compiler_params=pltpu.CompilerParams(vmem_limit_bytes=VMEM),
         name=f"edges_{f}",
     )(grid, grid, before, after, slope)
 
@@ -369,8 +388,9 @@
     rad, lm = lax.axis_size("rad"), lax.axis_size("lm")
     z = Sizes(rad * lm, grid_field, inverses, slot_blocks)
     choices = slot_choices(z)
-    kernels = z.local % 16 == 0 and z.blocks % GROUP == 0 and rad % 2 == 0 and lm == PLANE // 2
-    if not kernels or z.counts[z.degrees // 2 - 1] > choices[0]:
+    kernels = z.local % 16 == 0 and z.blocks % GROUP == 0 and rad % 4 == 0 and lm == PLANE // 2
+    low, high = z.counts[z.degrees // 2 - 1 : z.degrees // 2 + 1]
+    if not kernels or low + GIFT > choices[0] or high < GIFT or z.capacity - choices[0] > GIFT:
         return plain_body(z, grid_field, inverses, degree_start)
     me = lax.axis_index(AXES).reshape(1).astype(jnp.int32)
     choice, place = plan(z, degree_start, choices)
@@ -381,13 +401,19 @@
 def route(z, slots, grid_field, inverses, degree_start, me, place):
     (sent_0,) = pack(z, place, grid_field, 0, slots, False)
     sent_1, holder = pack(z, place, grid_field, 1, slots, True)
-    straight = lax.optimization_barrier((sent_1, *straight_inverses(inverses)))
-    columns = [exchange(z, sent, slots) for sent in (sent_0, straight[0])]
-    pieces = lax.optimization_barrier(plane_inverses(*straight[1:]))
-    solved = [
-        solve(z, holder, degree_start, me, columns[f], inverses, pieces, f, slots)
-        for f in range(z.fields)
-    ]
+    sent_1, own, across, along, far = lax.optimization_barrier(
+        (sent_1, *straight_inverses(inverses))
+    )
+    columns = [exchange(z, sent, slots) for sent in (sent_0, sent_1)]
+    corner_0 = swap(across[:1], "rad", 1)
+    even = [own, across, along]
+    odd = other_core(even)
+    pieces = lax.optimization_barrier((*even, corner_0, *odd, *other_core([corner_0]), far))
+    solved_0 = solve(z, holder, degree_start, me, columns[0], inverses, pieces, 0, slots)
+    corner_1 = swap(along[1:], "lm", 2)
+    pieces = (*even, corner_1, *odd, *other_core([corner_1]), far)
+    solved_1 = solve(z, holder, degree_start, me, columns[1], inverses, pieces, 1, slots)
+    solved = [solved_0, solved_1]
     returned = [
         exchange(z, solved[f], slots).reshape(z.devices * slots, z.local, z.width)
         for f in range(z.fields)

time: 282 us -> 268 us (0.950)
  waiting for transfers between devices: 182 us -> 171 us
  local copies, waits for them, and re-layouts: 7.05 us -> 0.15 us
    all_to_all x4, waiting for transfers between devices: 56 us -> 14.9 us  [exchange(): return lax.all_to_all(shaped, AXES, split_axis=0, concat_axis=0, tiled=True)]
    ppermute x9, waiting for transfers between devices: 73 us -> 107 us  [swap(): return lax.ppermute(value, axis, [(i, i ^ bit) for i in range(size)])]
    cond x24 -> x6, local copies, waits for them, and re-layouts: 6.91 us -> 0.01 us
    ppermute x4, waiting for transfers between devices: 52.7 us -> 49.8 us  [beside(): return (lax.ppermute(last, AXES, up), lax.ppermute(first, AXES, down))]
  transfers between devices with their start and end apart: 17 -> 18, of which waited for: 11 -> 12; matrix products, arithmetic and copies ran while one was open for 0% -> 0% of each run, Pallas kernels for 12% -> 13%
where the time goes in v1:
time: 268 us; the launch traced here: 267 us
  waiting for transfers between devices  171 us (64%)
  Pallas kernels  49 us (18%)
  starting transfers between devices  44.9 us (17%)
    ppermute x9, waiting for transfers between devices, swap(): return lax.ppermute(value, axis, [(i, i ^ bit) for i in range(size)])  107 us
    ppermute x4, waiting for transfers between devices, beside(): return (lax.ppermute(last, AXES, up), lax.ppermute(first, AXES, down))  49.8 us
    all_to_all x4, starting transfers between devices, exchange(): return lax.all_to_all(shaped, AXES, split_axis=0, concat_axis=0, tiled=True)  26.9 us
    pallas_call x2, Pallas kernels, solve(): pl.pallas_call(functools.partial(solve_kernel, z, f, slots, per_step), gr...  18.1 us
    all_to_all x4, waiting for transfers between devices, exchange(): return lax.all_to_all(shaped, AXES, split_axis=0, concat_axis=0, tiled=True)  14.9 us
    pallas_call x2, Pallas kernels, pack(): pl.pallas_call(functools.partial(pack_kernel, z), grid_spec=pltpu.Prefetc...  14.3 us
    ppermute x4, starting transfers between devices, beside(): return (lax.ppermute(last, AXES, up), lax.ppermute(first, AXES, down))  12.1 us
    pallas_call x2, Pallas kernels, unpack(): pl.pallas_call(functools.partial(unpack_kernel, z), grid_spec=pltpu.Prefe...  9.72 us
  transfers between devices with their start and end apart: 18, of which 12 were waited for; matrix products, arithmetic and copies ran while one was open for 0% of the time, Pallas kernels for 13%

profile of v1, /device:TPU:15, one launch (start us, length us, event | category | flops | bytes accessed | tf_op | source)
XLA Modules:
  0.0 267.5 jit_solution(6882109417608007)
XLA Ops:
  0.6 3.3 %plan.1 = (s32[1]{0:T(128)}, s32[544]{0:T(1024)S(1)}) custom-call(s32[64]{0:T(128)} %start_ref.1), custom_call_target="tpu_custom_call" | custom-call | tf_op jit(solution)/shard_map/plan/pallas_call | solution.py:105
  4.6 262.7 %conditional.1 = (bf16[2,16,544,128]{3,2,1,0:T(8,128)(2,1)}, bf16[2,16,544,128]{3,2,1,0:T(8,128)(2,1)}) conditional(s32[]{:T(128)} %bitcast.30, (s32[544]{0:T(1024)S(1)}, bf16[2,16,544,128]{3,2,1,0:T(8,128)(2,1)}, bf16[2,2,512,512]{3,2,1,0:T(8,128)(2,1)}, s32[64]{0:T(128)}, s32[]{:T(128)}, /*index=5*/s32[]{:T(128)}, ...), branch_computations={%region_0.0_spmd, %region_1.0_spmd, %region_2.0_spmd, %region_3.0_... | conditional | flops 24000000000 | bytes 150310416 | solution.py:398
  4.6 4.6 %pack_0.6 = bf16[576,16,128]{2,1,0:T(8,128)(2,1)} custom-call(s32[544]{0:T(1024)S(1)} %get-tuple-element.79.place_ref, bf16[2,16,544,128]{3,2,1,0:T(8,128)(2,1)} %get-tuple-element.218.field_ref), custom_call_target="tpu_custom_call" | custom-call | flops 1000000000 | bytes 10000000 | tf_op jit(solution)/shard_map/cond/branch_1_fun/pack_0/pallas_call | solution.py:182
  9.2 6.3 %all-to-all-start.6 = ((bf16[32,18,16,128]{3,2,1,0:T(8,128)(2,1)}), bf16[32,18,16,128]{3,2,1,0:T(8,128)(2,1)}, u32[]{:S(2)}, u32[]{:S(2)}) async-start(bf16[32,18,16,128]{3,2,1,0:T(8,128)(2,1)} %bitcast.10), calls=%async_computation.6 | async-start | bytes 4718592 | tf_op jit(solution)/shard_map/cond/branch_1_fun/all_to_all | solution.py:384
  15.6 0.0 copy-done.1
  15.6 0.1 slice_bitcast_fusion.1.rest_0_
  15.7 0.7 collective-permute-start.16
  16.4 0.3 collective-permute-start.15
  16.7 0.3 collective-permute-start.14
  17.0 9.7 %pack_1.6 = (bf16[576,16,128]{2,1,0:T(8,128)(2,1)}, s32[768]{0:T(1024)S(1)}) custom-call(s32[544]{0:T(1024)S(1)} %get-tuple-element.79.place_ref, bf16[2,16,544,128]{3,2,1,0:T(8,128)(2,1)} %get-tuple-element.218.field_ref), custom_call_target="tpu_custom_call" | custom-call | flops 1000000000 | bytes 10000000 | tf_op jit(solution)/shard_map/cond/branch_1_fun/pack_1/pallas_call | solution.py:182
  26.7 0.0 collective-permute-done.16.rest_8_
  26.8 38.2 %collective-permute-done.15.rest_2_ = bf16[2,512,512]{2,1,0:T(8,128)(2,1)S(1)} collective-permute-done((bf16[2,512,512]{2,1,0:T(8,128)(2,1)S(1)}, bf16[2,512,512]{2,1,0:T(8,128)(2,1)S(1)}, u32[]{:S(2)}, u32[]{:S(2)}) %collective-permute-start.15) | collective-permute-done | bytes 1048608 | tf_op jit(solution)/shard_map/cond/branch_1_fun/ppermute | solution.py:125
  64.9 0.0 collective-permute-done.14.rest_1_
  65.0 2.6 all-to-all-done.6.columns_ref
  67.5 6.9 %all-to-all-start.4 = ((bf16[32,18,16,128]{3,2,1,0:T(8,128)(2,1)}), bf16[32,18,16,128]{3,2,1,0:T(8,128)(2,1)}, u32[]{:S(2)}, u32[]{:S(2)}) async-start(bf16[32,18,16,128]{3,2,1,0:T(8,128)(2,1)} %bitcast.8), calls=%async_computation.4 | async-start | bytes 4718592 | tf_op jit(solution)/shard_map/cond/branch_1_fun/all_to_all | solution.py:384
  74.5 0.3 collective-permute-start.22
  74.8 0.6 collective-permute-start.19
  75.4 0.0 collective-permute-start.18
  75.4 0.5 collective-permute-start.20
  76.0 32.6 %collective-permute-done.22.rest_3_ = bf16[1,512,512]{2,1,0:T(8,128)(2,1)} collective-permute-done((bf16[1,512,512]{2,1,0:T(8,128)(2,1)S(1)}, bf16[1,512,512]{2,1,0:T(8,128)(2,1)}, u32[]{:S(2)}, u32[]{:S(2)}) %collective-permute-start.22) | collective-permute-done | bytes 524320 | tf_op jit(solution)/shard_map/cond/branch_1_fun/ppermute | solution.py:125
  108.6 0.4 collective-permute-start.23
  109.0 1.9 collective-permute-done.23.rest_7_
  110.9 0.0 collective-permute-done.18.rest_4_
  110.9 0.0 collective-permute-done.19.rest_5_
  110.9 0.0 collective-permute-done.20.rest_6_
  110.9 9.2 %solve_0.6 = bf16[32,18,16,128]{3,2,1,0:T(8,128)(2,1)} custom-call(s32[768]{0:T(1024)S(1)} %get-tuple-element.81.holder_ref, s32[64]{0:T(128)S(1)} %copy-done.11, s32[1]{0:T(128)} %bitcast.6.me_ref, bf16[32,18,16,128]{3,2,1,0:T(8,128)(2,1)} %all-to-all-done.6.columns_ref, bf16[2,2,512,512]{3,2,1,0:T(8,128)(2,1)} %get-tuple-element.256.inverses_ref, ...), custom_call_target="tpu_custom_call" | custom-call | flops 10000000000 | bytes 10000000 | tf_op jit(solution)/shard_map/cond/branch_1_fun/solve_0/pallas_call | solution.py:264
  120.2 6.0 %all-to-all-done.4.columns_ref = bf16[32,18,16,128]{3,2,1,0:T(8,128)(2,1)} async-done(((bf16[32,18,16,128]{3,2,1,0:T(8,128)(2,1)}), bf16[32,18,16,128]{3,2,1,0:T(8,128)(2,1)}, u32[]{:S(2)}, u32[]{:S(2)}) %all-to-all-start.4) | async-done | bytes 2359328 | tf_op jit(solution)/shard_map/cond/branch_1_fun/all_to_all | solution.py:384
  126.2 6.9 %all-to-all-start.7 = ((bf16[32,18,16,128]{3,2,1,0:T(8,128)(2,1)}), bf16[32,18,16,128]{3,2,1,0:T(8,128)(2,1)}, u32[]{:S(2)}, u32[]{:S(2)}) async-start(bf16[32,18,16,128]{3,2,1,0:T(8,128)(2,1)} %solve_0.6), calls=%async_computation.7 | async-start | bytes 4718592 | tf_op jit(solution)/shard_map/cond/branch_1_fun/all_to_all | solution.py:384
  133.1 0.3 collective-permute-start.17
  133.5 32.3 %collective-permute-done.17.rest_3_ = bf16[1,512,512]{2,1,0:T(8,128)(2,1)S(1)} collective-permute-done((bf16[1,512,512]{2,1,0:T(8,128)(2,1)S(1)}, bf16[1,512,512]{2,1,0:T(8,128)(2,1)S(1)}, u32[]{:S(2)}, u32[]{:S(2)}) %collective-permute-start.17) | collective-permute-done | bytes 524320 | tf_op jit(solution)/shard_map/cond/branch_1_fun/ppermute | solution.py:125
  165.8 2.3 collective-permute-start.21
  168.0 1.5 collective-permute-done.21.rest_7_
  169.6 8.9 %solve_1.6 = bf16[32,18,16,128]{3,2,1,0:T(8,128)(2,1)} custom-call(s32[768]{0:T(1024)S(1)} %get-tuple-element.81.holder_ref, s32[64]{0:T(128)S(1)} %copy-done.11, s32[1]{0:T(128)} %bitcast.6.me_ref, bf16[32,18,16,128]{3,2,1,0:T(8,128)(2,1)} %all-to-all-done.4.columns_ref, bf16[2,2,512,512]{3,2,1,0:T(8,128)(2,1)} %get-tuple-element.256.inverses_ref, ...), custom_call_target="tpu_custom_call" | custom-call | flops 10000000000 | bytes 10000000 | tf_op jit(solution)/shard_map/cond/branch_1_fun/solve_1/pallas_call | solution.py:264
  178.5 6.3 %all-to-all-done.7 = bf16[32,18,16,128]{3,2,1,0:T(8,128)(2,1)} async-done(((bf16[32,18,16,128]{3,2,1,0:T(8,128)(2,1)}), bf16[32,18,16,128]{3,2,1,0:T(8,128)(2,1)}, u32[]{:S(2)}, u32[]{:S(2)}) %all-to-all-start.7) | async-done | bytes 2359328 | tf_op jit(solution)/shard_map/cond/branch_1_fun/all_to_all | solution.py:384
  184.8 6.8 %all-to-all-start.5 = ((bf16[32,18,16,128]{3,2,1,0:T(8,128)(2,1)}), bf16[32,18,16,128]{3,2,1,0:T(8,128)(2,1)S(1)}, u32[]{:S(2)}, u32[]{:S(2)}) async-start(bf16[32,18,16,128]{3,2,1,0:T(8,128)(2,1)} %solve_1.6), calls=%async_computation.5 | async-start | bytes 4718592 | tf_op jit(solution)/shard_map/cond/branch_1_fun/all_to_all | solution.py:384
  191.7 5.7 %unpack_0.6 = (bf16[2,16,544,128]{3,2,1,0:T(8,128)(2,1)}, bf16[2,16,544,128]{3,2,1,0:T(8,128)(2,1)}, bf16[1,544,128]{2,1,0:T(8,128)(2,1)}, bf16[1,544,128]{2,1,0:T(8,128)(2,1)}) custom-call(s32[544]{0:T(1024)S(1)} %get-tuple-element.79.place_ref, bf16[576,16,128]{2,1,0:T(8,128)(2,1)} %bitcast.11.returned_ref), custom_call_target="tpu_custom_call" | custom-call | flops 1000000000 | bytes 10000000 | tf_op jit(solution)/shard_map/cond/branch_1_fun/unpack_0/pallas_call | solution.py:316
  197.4 3.3 %collective-permute-start.24 = (bf16[1,544,128]{2,1,0:T(8,128)(2,1)}, bf16[1,544,128]{2,1,0:T(8,128)(2,1)S(1)}, u32[]{:S(2)}, u32[]{:S(2)}) collective-permute-start(bf16[1,544,128]{2,1,0:T(8,128)(2,1)} %get-tuple-element.101), channel_id=1, source_target_pairs={{0,1},{1,2},{2,3},{3,4},{4,5},{5,6},{6,7},{7,8},{8,9},{9,10},{10,1... | collective-permute-start | bytes 417800 | tf_op jit(solution)/shard_map/cond/branch_1_fun/ppermute | solution.py:379
  200.8 1.9 collective-permute-start.25
  202.7 42.3 %collective-permute-done.24.before_ref = bf16[1,544,128]{2,1,0:T(8,128)(2,1)S(1)} collective-permute-done((bf16[1,544,128]{2,1,0:T(8,128)(2,1)}, bf16[1,544,128]{2,1,0:T(8,128)(2,1)S(1)}, u32[]{:S(2)}, u32[]{:S(2)}) %collective-permute-start.24) | collective-permute-done | bytes 139296 | tf_op jit(solution)/shard_map/cond/branch_1_fun/ppermute | solution.py:379
  245.0 1.2 collective-permute-done.25.after_ref
  246.2 1.7 edges_0.6.rest_1_
  247.9 0.0 all-to-all-done.5
  248.0 4.0 %unpack_1.6 = (bf16[2,16,544,128]{3,2,1,0:T(8,128)(2,1)}, bf16[2,16,544,128]{3,2,1,0:T(8,128)(2,1)}, bf16[1,544,128]{2,1,0:T(8,128)(2,1)S(1)}, bf16[1,544,128]{2,1,0:T(8,128)(2,1)S(1)}) custom-call(s32[544]{0:T(1024)S(1)} %get-tuple-element.79.place_ref, bf16[576,16,128]{2,1,0:T(8,128)(2,1)S(1)} %bitcast.39, ...), custom_call_target="tpu_custom_call", output_to_operand_aliasing={{0}: (2, {}), {1}: (3, {})} | custom-call | flops 1000000000 | bytes 10000000 | tf_op jit(solution)/shard_map/cond/branch_1_fun/unpack_1/pallas_call | solution.py:316
  251.9 4.9 %collective-permute-start.26 = (bf16[1,544,128]{2,1,0:T(8,128)(2,1)S(1)}, bf16[1,544,128]{2,1,0:T(8,128)(2,1)S(1)}, u32[]{:S(2)}, u32[]{:S(2)}) collective-permute-start(bf16[1,544,128]{2,1,0:T(8,128)(2,1)S(1)} %get-tuple-element.105), channel_id=1, source_target_pairs={{0,1},{1,2},{2,3},{3,4},{4,5},{5,6},{6,7},{7,8},{8,9},{9,10},{10,1... | collective-permute-start | bytes 417800 | tf_op jit(solution)/shard_map/cond/branch_1_fun/ppermute | solution.py:379
  256.8 1.9 collective-permute-start.27
  258.8 0.1 collective-permute-done.26.before_ref
  258.8 6.2 %collective-permute-done.27.after_ref = bf16[1,544,128]{2,1,0:T(8,128)(2,1)S(1)} collective-permute-done((bf16[1,544,128]{2,1,0:T(8,128)(2,1)S(1)}, bf16[1,544,128]{2,1,0:T(8,128)(2,1)S(1)}, u32[]{:S(2)}, u32[]{:S(2)}) %collective-permute-start.27) | collective-permute-done | bytes 139296 | tf_op jit(solution)/shard_map/cond/branch_1_fun/ppermute | solution.py:379
  265.0 1.7 edges_1.6
  (7 shorter events, 0.1 us)
Async XLA Ops:
  9.2 6.3 %copy-start.1 = (bf16[2,2,512,512]{3,2,1,0:T(8,128)(2,1)S(1)}, bf16[2,2,512,512]{3,2,1,0:T(8,128)(2,1)}, u32[]{:S(2)}) copy-start(bf16[2,2,512,512]{3,2,1,0:T(8,128)(2,1)} %get-tuple-element.256.inverses_ref) | copy-start | bytes 6291460 | tf_op jit(solution)/shard_map/cond
  9.2 58.3 %all-to-all-start.6 = ((bf16[32,18,16,128]{3,2,1,0:T(8,128)(2,1)}), bf16[32,18,16,128]{3,2,1,0:T(8,128)(2,1)}, u32[]{:S(2)}, u32[]{:S(2)}) async-start(bf16[32,18,16,128]{3,2,1,0:T(8,128)(2,1)} %bitcast.10), calls=%async_computation.6 | async-start | bytes 4718592 | tf_op jit(solution)/shard_map/cond/branch_1_fun/all_to_all | solution.py:384
  15.7 11.1 %collective-permute-start.16 = (bf16[2,512,512]{2,1,0:T(8,128)(2,1)S(1)}, bf16[2,512,512]{2,1,0:T(8,128)(2,1)S(1)}, u32[]{:S(2)}, u32[]{:S(2)}) collective-permute-start(bf16[2,512,512]{2,1,0:T(8,128)(2,1)S(1)} %slice_bitcast_fusion.1.rest_0_), channel_id=1, source_target_pairs={{0,8},{2,10},{4,12},{6,14},{8,0},{10,2},{12,4},{14,6},{16,24},{18,... | collective-permute-start | bytes 3145736 | tf_op jit(solution)/shard_map/cond/branch_1_fun/ppermute | solution.py:132
  16.4 48.6 %collective-permute-start.15 = (bf16[2,512,512]{2,1,0:T(8,128)(2,1)S(1)}, bf16[2,512,512]{2,1,0:T(8,128)(2,1)S(1)}, u32[]{:S(2)}, u32[]{:S(2)}) collective-permute-start(bf16[2,512,512]{2,1,0:T(8,128)(2,1)S(1)} %slice_bitcast_fusion.1.rest_0_), channel_id=1, source_target_pairs={{0,4},{4,0},{8,12},{12,8},{16,20},{20,16},{24,28},{28,24},{1,5},{5... | collective-permute-start | bytes 3145736 | tf_op jit(solution)/shard_map/cond/branch_1_fun/ppermute | solution.py:125
  16.7 48.2 %collective-permute-start.14 = (bf16[2,512,512]{2,1,0:T(8,128)(2,1)S(1)}, bf16[2,512,512]{2,1,0:T(8,128)(2,1)S(1)}, u32[]{:S(2)}, u32[]{:S(2)}) collective-permute-start(bf16[2,512,512]{2,1,0:T(8,128)(2,1)S(1)} %slice_bitcast_fusion.1.rest_0_), channel_id=1, source_target_pairs={{0,2},{1,3},{2,0},{3,1},{4,6},{5,7},{6,4},{7,5},{8,10},{9,11},{10,... | collective-permute-start | bytes 3145736 | tf_op jit(solution)/shard_map/cond/branch_1_fun/ppermute | solution.py:125
  26.7 38.2 %copy-start.6 = (bf16[2,512,512]{2,1,0:T(8,128)(2,1)}, bf16[2,512,512]{2,1,0:T(8,128)(2,1)S(1)}, u32[]{:S(2)}) copy-start(bf16[2,512,512]{2,1,0:T(8,128)(2,1)S(1)} %collective-permute-done.16.rest_8_) | copy-start | bytes 3145732 | tf_op jit(solution)/shard_map/cond
  67.5 43.4 %copy-start.11 = (s32[64]{0:T(128)S(1)}, s32[64]{0:T(128)}, u32[]{:S(2)}) copy-start(s32[64]{0:T(128)} %get-tuple-element.82.start_ref) | copy-start | bytes 772 | tf_op jit(solution)/shard_map/cond
  67.5 58.7 %all-to-all-start.4 = ((bf16[32,18,16,128]{3,2,1,0:T(8,128)(2,1)}), bf16[32,18,16,128]{3,2,1,0:T(8,128)(2,1)}, u32[]{:S(2)}, u32[]{:S(2)}) async-start(bf16[32,18,16,128]{3,2,1,0:T(8,128)(2,1)} %bitcast.8), calls=%async_computation.4 | async-start | bytes 4718592 | tf_op jit(solution)/shard_map/cond/branch_1_fun/all_to_all | solution.py:384
  74.5 34.1 %collective-permute-start.22 = (bf16[1,512,512]{2,1,0:T(8,128)(2,1)S(1)}, bf16[1,512,512]{2,1,0:T(8,128)(2,1)}, u32[]{:S(2)}, u32[]{:S(2)}) collective-permute-start(bf16[1,512,512]{2,1,0:T(8,128)(2,1)S(1)} %slice.35), channel_id=1, source_target_pairs={{0,4},{4,0},{8,12},{12,8},{16,20},{20,16},{24,28},{28,24},{1,5},{5... | collective-permute-start | bytes 1572872 | tf_op jit(solution)/shard_map/cond/branch_1_fun/ppermute | solution.py:125
  74.8 36.1 %collective-permute-start.19 = (bf16[2,512,512]{2,1,0:T(8,128)(2,1)S(1)}, bf16[2,512,512]{2,1,0:T(8,128)(2,1)}, u32[]{:S(2)}, u32[]{:S(2)}) collective-permute-start(bf16[2,512,512]{2,1,0:T(8,128)(2,1)S(1)} %collective-permute-done.14.rest_1_), channel_id=1, source_target_pairs={{0,1},{1,0},{2,3},{3,2},{4,5},{5,4},{6,7},{7,6},{8,9},{9,8},{10,11... | collective-permute-start | bytes 3145736 | tf_op jit(solution)/shard_map/cond/branch_1_fun/ppermute | solution.py:125
  75.4 35.5 %collective-permute-start.18 = (bf16[2,512,512]{2,1,0:T(8,128)(2,1)S(1)}, bf16[2,512,512]{2,1,0:T(8,128)(2,1)}, u32[]{:S(2)}, u32[]{:S(2)}) collective-permute-start(bf16[2,512,512]{2,1,0:T(8,128)(2,1)S(1)} %slice_bitcast_fusion.1.rest_0_), channel_id=1, source_target_pairs={{0,1},{1,0},{2,3},{3,2},{4,5},{5,4},{6,7},{7,6},{8,9},{9,8},{10,11... | collective-permute-start | bytes 3145736 | tf_op jit(solution)/shard_map/cond/branch_1_fun/ppermute | solution.py:125
  75.4 35.5 %collective-permute-start.20 = (bf16[2,512,512]{2,1,0:T(8,128)(2,1)S(1)}, bf16[2,512,512]{2,1,0:T(8,128)(2,1)}, u32[]{:S(2)}, u32[]{:S(2)}) collective-permute-start(bf16[2,512,512]{2,1,0:T(8,128)(2,1)S(1)} %collective-permute-done.15.rest_2_), channel_id=1, source_target_pairs={{0,1},{1,0},{2,3},{3,2},{4,5},{5,4},{6,7},{7,6},{8,9},{9,8},{10,11... | collective-permute-start | bytes 3145736 | tf_op jit(solution)/shard_map/cond/branch_1_fun/ppermute | solution.py:125
  108.6 2.3 collective-permute-start.23
  126.2 58.7 %all-to-all-start.7 = ((bf16[32,18,16,128]{3,2,1,0:T(8,128)(2,1)}), bf16[32,18,16,128]{3,2,1,0:T(8,128)(2,1)}, u32[]{:S(2)}, u32[]{:S(2)}) async-start(bf16[32,18,16,128]{3,2,1,0:T(8,128)(2,1)} %solve_0.6), calls=%async_computation.7 | async-start | bytes 4718592 | tf_op jit(solution)/shard_map/cond/branch_1_fun/all_to_all | solution.py:384
  133.1 32.6 %collective-permute-start.17 = (bf16[1,512,512]{2,1,0:T(8,128)(2,1)S(1)}, bf16[1,512,512]{2,1,0:T(8,128)(2,1)S(1)}, u32[]{:S(2)}, u32[]{:S(2)}) collective-permute-start(bf16[1,512,512]{2,1,0:T(8,128)(2,1)S(1)} %slice.34), channel_id=1, source_target_pairs={{0,2},{1,3},{2,0},{3,1},{4,6},{5,7},{6,4},{7,5},{8,10},{9,11},{10,... | collective-permute-start | bytes 1572872 | tf_op jit(solution)/shard_map/cond/branch_1_fun/ppermute | solution.py:125
  165.8 3.8 %collective-permute-start.21 = (bf16[1,512,512]{2,1,0:T(8,128)(2,1)S(1)}, bf16[1,512,512]{2,1,0:T(8,128)(2,1)S(1)}, u32[]{:S(2)}, u32[]{:S(2)}) collective-permute-start(bf16[1,512,512]{2,1,0:T(8,128)(2,1)S(1)} %collective-permute-done.17.rest_3_), channel_id=1, source_target_pairs={{0,1},{1,0},{2,3},{3,2},{4,5},{5,4},{6,7},{7,6},{8,9},{9,8},{10,11... | collective-permute-start | bytes 1572872 | tf_op jit(solution)/shard_map/cond/branch_1_fun/ppermute | solution.py:125
  184.8 63.1 %all-to-all-start.5 = ((bf16[32,18,16,128]{3,2,1,0:T(8,128)(2,1)}), bf16[32,18,16,128]{3,2,1,0:T(8,128)(2,1)S(1)}, u32[]{:S(2)}, u32[]{:S(2)}) async-start(bf16[32,18,16,128]{3,2,1,0:T(8,128)(2,1)} %solve_1.6), calls=%async_computation.5 | async-start | bytes 4718592 | tf_op jit(solution)/shard_map/cond/branch_1_fun/all_to_all | solution.py:384
  197.4 47.6 %collective-permute-start.24 = (bf16[1,544,128]{2,1,0:T(8,128)(2,1)}, bf16[1,544,128]{2,1,0:T(8,128)(2,1)S(1)}, u32[]{:S(2)}, u32[]{:S(2)}) collective-permute-start(bf16[1,544,128]{2,1,0:T(8,128)(2,1)} %get-tuple-element.101), channel_id=1, source_target_pairs={{0,1},{1,2},{2,3},{3,4},{4,5},{5,6},{6,7},{7,8},{8,9},{9,10},{10,1... | collective-permute-start | bytes 417800 | tf_op jit(solution)/shard_map/cond/branch_1_fun/ppermute | solution.py:379
  200.8 45.4 %collective-permute-start.25 = (bf16[1,544,128]{2,1,0:T(8,128)(2,1)}, bf16[1,544,128]{2,1,0:T(8,128)(2,1)S(1)}, u32[]{:S(2)}, u32[]{:S(2)}) collective-permute-start(bf16[1,544,128]{2,1,0:T(8,128)(2,1)} %get-tuple-element.102), channel_id=1, source_target_pairs={{1,0},{2,1},{3,2},{4,3},{5,4},{6,5},{7,6},{8,7},{9,8},{10,9},{11,1... | collective-permute-start | bytes 417800 | tf_op jit(solution)/shard_map/cond/branch_1_fun/ppermute | solution.py:379
  251.9 6.9 %collective-permute-start.26 = (bf16[1,544,128]{2,1,0:T(8,128)(2,1)S(1)}, bf16[1,544,128]{2,1,0:T(8,128)(2,1)S(1)}, u32[]{:S(2)}, u32[]{:S(2)}) collective-permute-start(bf16[1,544,128]{2,1,0:T(8,128)(2,1)S(1)} %get-tuple-element.105), channel_id=1, source_target_pairs={{0,1},{1,2},{2,3},{3,4},{4,5},{5,6},{6,7},{7,8},{8,9},{9,10},{10,1... | collective-permute-start | bytes 417800 | tf_op jit(solution)/shard_map/cond/branch_1_fun/ppermute | solution.py:379
  256.8 8.2 %collective-permute-start.27 = (bf16[1,544,128]{2,1,0:T(8,128)(2,1)S(1)}, bf16[1,544,128]{2,1,0:T(8,128)(2,1)S(1)}, u32[]{:S(2)}, u32[]{:S(2)}) collective-permute-start(bf16[1,544,128]{2,1,0:T(8,128)(2,1)S(1)} %get-tuple-element.106), channel_id=1, source_target_pairs={{1,0},{2,1},{3,2},{4,3},{5,4},{6,5},{7,6},{8,7},{9,8},{10,9},{11,1... | collective-permute-start | bytes 417800 | tf_op jit(solution)/shard_map/cond/branch_1_fun/ppermute | solution.py:379

commit v2 on v1

--- a/solution.py
+++ b/solution.py
@@ -15,6 +15,7 @@
 GIFT = 8
 GROUP = 16
 VMEM = 48 << 20
+RIDES = 8
 
 inner_radius = 0.35
 shell_depth = 0.65
@@ -33,6 +34,15 @@
         index = np.arange(self.degrees)
         self.counts = [int(c) for c in index // self.group_size + 1]
         self.starts = [int(s) for s in np.cumsum(self.counts) - self.counts]
+        self.partial = [q for q in range(self.degrees) if (q + 1) % self.group_size]
+
+    def last_block(self, q):
+        turns = lax.div(q, self.group_size)
+        rest = lax.rem(q, self.group_size)
+        return self.group_size * lax.div(turns * (turns + 1), 2) + rest * (turns + 1) + turns
+
+    def last_live(self, q):
+        return 2 * self.spacing * (lax.rem(q, self.group_size) + 1)
 
 
 def slot_choices(z):
@@ -40,12 +50,40 @@
     return sorted({min(mean + extra, z.capacity) for extra in (0, 1, 2, 3)} | {z.capacity})
 
 
-def plan_kernel(z, choices, start_ref, choice_ref, place_ref, load_ref, room_ref, device_ref, next_ref):
+def plan_kernel(z, choices, start_ref, choice_ref, place_ref, mate_ref, load_ref, room_ref, device_ref,
+                next_ref, count_ref, stack_ref):
     half = z.degrees // 2
     planes = z.devices // PLANE
     owner = [lax.div(start_ref[q], z.capacity) for q in range(z.degrees)]
     for q in range(half, z.degrees):
         load_ref[owner[q]] = start_ref[q] - owner[q] * z.capacity + z.counts[q]
+    kinds = z.group_size
+    for i in range(planes * kinds):
+        count_ref[i] = 0
+    for q in range(z.degrees):
+        mate_ref[q] = -1
+    for q in z.partial:
+        if q < half:
+            kind = lax.div(owner[q], PLANE) * kinds + q % kinds
+            stack_ref[kind * PLANE + count_ref[kind]] = q
+            count_ref[kind] += 1
+    for q in sorted(z.partial, key=lambda q: -(q % kinds)):
+        if q < half:
+            continue
+        first_kind = lax.div(owner[q], PLANE) * kinds
+        kind = jnp.int32(-1)
+        for i in range(kinds - 1 - q % kinds):
+            kind = jnp.where(count_ref[first_kind + i] > 0, first_kind + i, kind)
+
+        @pl.when(kind >= 0)
+        def _(kind=kind, q=q):
+            left = count_ref[kind] - 1
+            count_ref[kind] = left
+            host = stack_ref[kind * PLANE + left]
+            mate_ref[q] = host
+            mate_ref[host] = q
+            load_ref[owner[q]] -= 1
+
     loads = [load_ref[d] for d in range(z.devices)]
     totals = [sum(loads[g * PLANE : (g + 1) * PLANE]) for g in range(planes)]
     most = functools.reduce(jnp.maximum, [totals[g] + totals[g + 1] for g in range(0, planes, 2)])
@@ -96,7 +134,13 @@
             place_ref[z.starts[q] + p] = given + p
             return carry
 
-        lax.fori_loop(kept, z.counts[q], give, 0)
+        host = mate_ref[q]
+        lax.fori_loop(kept, z.counts[q] - jnp.where(host >= 0, 1, 0), give, 0)
+
+        @pl.when(host >= 0)
+        def _(host=host, q=q):
+            home = start_ref[host] + lax.div(start_ref[host], z.capacity) * (slots - z.capacity)
+            place_ref[z.starts[q] + z.counts[q] - 1] = home + lax.div(host, kinds)
 
 
 def plan(z, degree_start, choices):
@@ -105,16 +149,19 @@
     return pl.pallas_call(
         functools.partial(plan_kernel, z, choices),
         in_specs=[smem],
-        out_specs=[smem] * 2,
+        out_specs=[smem] * 3,
         out_shape=[
             jax.ShapeDtypeStruct((1,), jnp.int32),
             jax.ShapeDtypeStruct((z.blocks,), jnp.int32),
+            jax.ShapeDtypeStruct((z.degrees,), jnp.int32),
         ],
         scratch_shapes=[
             pltpu.SMEM((z.devices,), jnp.int32),
             pltpu.SMEM((z.devices,), jnp.int32),
             pltpu.SMEM((planes,), jnp.int32),
             pltpu.SMEM((planes,), jnp.int32),
+            pltpu.SMEM((planes * z.group_size,), jnp.int32),
+            pltpu.SMEM((planes * z.group_size * PLANE,), jnp.int32),
         ],
         name="plan",
     )(degree_start)
@@ -136,7 +183,14 @@
     return [swap(value, "lm", 1) for value in values]
 
 
-def pack_kernel(z, place_ref, field_ref, out_ref, *rest):
+def riding(z, mate_ref, q):
+    b, host = z.last_block(q), mate_ref[q]
+    rides = host >= 0
+    host = jnp.maximum(host, 0)
+    return b, jnp.where(rides, z.last_block(host), b), jnp.where(rides, z.last_live(host), z.width)
+
+
+def pack_kernel(z, place_ref, mate_ref, field_ref, out_ref, *rest):
     wide_ref = rest[-1]
     pitch = z.blocks + 1
     for level in range(z.local):
@@ -150,6 +204,16 @@
         return carry
 
     lax.fori_loop(0, z.blocks // GROUP, group, 0)
+    column = lax.broadcasted_iota(jnp.int32, (z.local, z.width), 1)
+
+    def ride(q, carry):
+        b, host_block, live = riding(z, mate_ref, q)
+        rider = pltpu.roll(wide_ref[pl.ds(b, z.local, stride=pitch), :], live, 1)
+        tile = wide_ref[pl.ds(host_block, z.local, stride=pitch), :]
+        out_ref[place_ref[b]] = jnp.where(column < live, tile, rider).astype(jnp.bfloat16)
+        return carry
+
+    lax.fori_loop(z.degrees // 2, z.degrees, ride, 0, unroll=RIDES)
     if len(rest) == 1:
         return
     holder_ref = rest[0]
@@ -166,13 +230,14 @@
             return inner
 
         count = lax.div(q, z.group_size) + 1
-        lax.fori_loop(0, count, block, 0)
+        rides = (q >= z.degrees // 2) & (mate_ref[q] >= 0)
+        lax.fori_loop(0, count - jnp.where(rides, 1, 0), block, 0)
         return b + count
 
     lax.fori_loop(0, z.degrees, degree, 0)
 
 
-def pack(z, place, grid_field, f, slots, with_holder):
+def pack(z, place, mate, grid_field, f, slots, with_holder):
     total = z.devices * slots
     out_specs = [pl.BlockSpec((total, z.local, z.width), lambda i, *s: (0, 0, 0))]
     out_shape = [jax.ShapeDtypeStruct((total, z.local, z.width), jnp.bfloat16)]
@@ -182,7 +247,7 @@
     return pl.pallas_call(
         functools.partial(pack_kernel, z),
         grid_spec=pltpu.PrefetchScalarGridSpec(
-            num_scalar_prefetch=1,
+            num_scalar_prefetch=2,
             grid=(1,),
             in_specs=[
                 pl.BlockSpec((1, z.local, z.blocks, z.width), lambda i, *s: (f, 0, 0, 0))
@@ -194,10 +259,10 @@
         compiler_params=pltpu.CompilerParams(vmem_limit_bytes=VMEM),
         cost_estimate=pl.CostEstimate(flops=10**9, bytes_accessed=10**7, transcendentals=0),
         name=f"pack_{f}",
-    )(place, grid_field)
-
-
-def solve_kernel(z, f, slots, per_step, holder_ref, start_ref, me_ref, columns_ref, inverses_ref, *rest):
+    )(place, mate, grid_field)
+
+
+def solve_kernel(z, f, slots, per_step, holder_ref, start_ref, mate_ref, me_ref, columns_ref, inverses_ref, *rest):
     (own, across, along, corner, own_odd, across_odd, along_odd, corner_odd, far) = rest[:9]
     out_ref, matrix_ref, square_ref, above_ref, below_ref, sems = rest[9:]
     strength = diffusion_numbers[f]
@@ -232,18 +297,26 @@
             copy.wait()
 
     column = lax.broadcasted_iota(jnp.int32, shape, 1)
-    for k in range(per_step):
-        slot = jnp.minimum(step * per_step + k, slots - 1)
-        code = holder_ref[me * slots + slot]
-        q = lax.div(code, OB)
+    host = lax.div(holder_ref[me * slots], OB)
+    rider = mate_ref[host]
+    host_at = lax.div(host, z.group_size) - step * per_step
+    rides = (rider >= 0) & (host_at >= 0) & (host_at < per_step)
+
+    def block(i, carry):
+        again = i >= per_step
+        k = jnp.where(again, host_at, i)
+        code = holder_ref[me * slots + jnp.minimum(step * per_step + k, slots - 1)]
+        q = jnp.where(again, rider, lax.div(code, OB))
         value = z.spacing * (q + 1) - 1
+        last = value - lax.rem(code, OB) * (z.width // 2)
+        begin = jnp.where(again, z.last_live(host), 0)
+        end = jnp.where(again, begin + z.last_live(rider), 2 * last + 2)
         offset = lax.div(start_ref[q], z.capacity) ^ me
         which = jnp.where(offset < PLANE, offset, PLANE + 1)
         which = jnp.where(q >= z.degrees // 2, which, PLANE)
         factor = (value * (value + 1)).astype(jnp.float32)
-        limit = 2 * (value - lax.rem(code, OB) * (z.width // 2)) + 1
         u = columns_ref[:, k].reshape(shape).astype(jnp.float32)
-        u = jnp.where(column <= limit, u, 0.0)
+        u = jnp.where((column >= begin) & (column < end), u, 0.0)
         weight = (1.0 - 2.0 * strength) - factor * square_ref[...]
         rhs = weight * u
         rhs += above_ref[...] * pltpu.roll(u, z.levels - 1, 0)
@@ -253,10 +326,15 @@
         both = jnp.concatenate([high, low], axis=1)
         product = jnp.dot(matrix_ref[which], both, preferred_element_type=jnp.float32)
         solved = product[:, : z.width] + product[:, z.width :]
-        out_ref[:, k] = solved.astype(jnp.bfloat16).reshape(z.devices, z.local, z.width)
-
-
-def solve(z, holder, degree_start, me, columns, inverses, pieces, f, slots):
+        earlier = out_ref[:, k].reshape(shape).astype(jnp.float32)
+        solved = jnp.where(column >= begin, solved, earlier).astype(jnp.bfloat16)
+        out_ref[:, k] = solved.reshape(z.devices, z.local, z.width)
+        return carry
+
+    lax.fori_loop(0, per_step + jnp.where(rides, 1, 0), block, 0)
+
+
+def solve(z, holder, degree_start, mate, me, columns, inverses, pieces, f, slots):
     steps = pl.cdiv(slots, 5)
     per_step = pl.cdiv(slots, steps)
     block = (z.devices, per_step, z.local, z.width)
@@ -264,7 +342,7 @@
     return pl.pallas_call(
         functools.partial(solve_kernel, z, f, slots, per_step),
         grid_spec=pltpu.PrefetchScalarGridSpec(
-            num_scalar_prefetch=3,
+            num_scalar_prefetch=4,
             grid=(steps,),
             in_specs=[spec] + [pl.BlockSpec(memory_space=pl.ANY)] * (1 + len(pieces)),
             out_specs=spec,
@@ -276,10 +354,10 @@
         compiler_params=pltpu.CompilerParams(vmem_limit_bytes=VMEM),
         cost_estimate=pl.CostEstimate(flops=10**10, bytes_accessed=10**7, transcendentals=0),
         name=f"solve_{f}",
-    )(holder, degree_start, me, columns, inverses, *pieces)
-
-
-def unpack_kernel(z, place_ref, returned_ref, *rest):
+    )(holder, degree_start, mate, me, columns, inverses, *pieces)
+
+
+def unpack_kernel(z, place_ref, mate_ref, returned_ref, *rest):
     grid_ref, slope_ref, first_ref, last_ref, wide_ref = rest[-5:]
     pitch = z.blocks + 1
 
@@ -291,6 +369,19 @@
         return carry
 
     lax.fori_loop(0, z.blocks // GROUP, gather, 0)
+    column = lax.broadcasted_iota(jnp.int32, (z.local, z.width), 1)
+
+    def ride(q, carry):
+        b, host_block, live = riding(z, mate_ref, q)
+        tile = returned_ref[place_ref[b]].astype(jnp.float32)
+        rider = pltpu.roll(tile, z.width - live, 1)
+        host_rows = pl.ds(host_block, z.local, stride=pitch)
+        wide_ref[host_rows, :] = jnp.where(column < live, tile, 0.0)
+        rows = pl.ds(b, z.local, stride=pitch)
+        wide_ref[rows, :] = jnp.where(column < z.last_live(q), rider, 0.0)
+        return carry
+
+    lax.fori_loop(z.degrees // 2, z.degrees, ride, 0, unroll=RIDES)
 
     def group(g, carry):
         at = pl.multiple_of(g * GROUP, GROUP)
@@ -308,7 +399,7 @@
     lax.fori_loop(0, z.blocks // GROUP, group, 0, unroll=2)
 
 
-def unpack(z, place, returned, f, earlier):
+def unpack(z, place, mate, returned, f, earlier):
     whole = jax.ShapeDtypeStruct((z.fields, z.local, z.blocks, z.width), jnp.bfloat16)
     level = jax.ShapeDtypeStruct((1, z.blocks, z.width), jnp.bfloat16)
     spec = pl.BlockSpec((1, z.local, z.blocks, z.width), lambda i, *s: (f, 0, 0, 0))
@@ -316,7 +407,7 @@
     return pl.pallas_call(
         functools.partial(unpack_kernel, z),
         grid_spec=pltpu.PrefetchScalarGridSpec(
-            num_scalar_prefetch=1,
+            num_scalar_prefetch=2,
             grid=(1,),
             in_specs=[pl.BlockSpec(returned.shape, lambda i, *s: (0, 0, 0))]
             + [pl.BlockSpec(memory_space=pl.ANY)] * len(earlier),
@@ -324,11 +415,11 @@
             scratch_shapes=[pltpu.VMEM((z.local * (z.blocks + 1), z.width), jnp.float32)],
         ),
         out_shape=[whole, whole, level, level],
-        input_output_aliases={2 + i: i for i in range(len(earlier))},
+        input_output_aliases={3 + i: i for i in range(len(earlier))},
         compiler_params=pltpu.CompilerParams(vmem_limit_bytes=VMEM if earlier else 60 << 20),
         cost_estimate=pl.CostEstimate(flops=10**9, bytes_accessed=10**7, transcendentals=0),
         name=f"unpack_{f}",
-    )(place, returned, *earlier)
+    )(place, mate, returned, *earlier)
 
 
 def edge_kernel(z, f, second_ref, before_last_ref, before_ref, after_ref, slope_in_ref, slope_ref,
@@ -390,17 +481,17 @@
     choices = slot_choices(z)
     kernels = z.local % 16 == 0 and z.blocks % GROUP == 0 and rad % 4 == 0 and lm == PLANE // 2
     low, high = z.counts[z.degrees // 2 - 1 : z.degrees // 2 + 1]
-    if not kernels or low + GIFT > choices[0] or high < GIFT or z.capacity - choices[0] > GIFT:
+    if not kernels or low + GIFT > choices[0] or high <= GIFT or z.capacity - choices[0] > GIFT:
         return plain_body(z, grid_field, inverses, degree_start)
     me = lax.axis_index(AXES).reshape(1).astype(jnp.int32)
-    choice, place = plan(z, degree_start, choices)
+    choice, place, mate = plan(z, degree_start, choices)
     routes = [functools.partial(route, z, slots) for slots in choices]
-    return lax.switch(choice[0], routes, grid_field, inverses, degree_start, me, place)
-
-
-def route(z, slots, grid_field, inverses, degree_start, me, place):
-    (sent_0,) = pack(z, place, grid_field, 0, slots, False)
-    sent_1, holder = pack(z, place, grid_field, 1, slots, True)
+    return lax.switch(choice[0], routes, grid_field, inverses, degree_start, me, place, mate)
+
+
+def route(z, slots, grid_field, inverses, degree_start, me, place, mate):
+    (sent_0,) = pack(z, place, mate, grid_field, 0, slots, False)
+    sent_1, holder = pack(z, place, mate, grid_field, 1, slots, True)
     sent_1, own, across, along, far = lax.optimization_barrier(
         (sent_1, *straight_inverses(inverses))
     )
@@ -409,10 +500,10 @@
     even = [own, across, along]
     odd = other_core(even)
     pieces = lax.optimization_barrier((*even, corner_0, *odd, *other_core([corner_0]), far))
-    solved_0 = solve(z, holder, degree_start, me, columns[0], inverses, pieces, 0, slots)
+    solved_0 = solve(z, holder, degree_start, mate, me, columns[0], inverses, pieces, 0, slots)
     corner_1 = swap(along[1:], "lm", 2)
     pieces = (*even, corner_1, *odd, *other_core([corner_1]), far)
-    solved_1 = solve(z, holder, degree_start, me, columns[1], inverses, pieces, 1, slots)
+    solved_1 = solve(z, holder, degree_start, mate, me, columns[1], inverses, pieces, 1, slots)
     solved = [solved_0, solved_1]
     returned = [
         exchange(z, solved[f], slots).reshape(z.devices * slots, z.local, z.width)
@@ -420,7 +511,7 @@
     ]
     outs = ()
     for f in range(z.fields):
-        grid, slope, first, last = unpack(z, place, returned[f], f, outs)
+        grid, slope, first, last = unpack(z, place, mate, returned[f], f, outs)
         outs = (grid, edges(z, slope, grid, *beside(z, first, last), f))
     return outs
 

time: 268 us -> 270 us (level)
  Pallas kernels: 49 us -> 60.5 us
  waiting for transfers between devices: 171 us -> 161 us
    all_to_all x4, waiting for transfers between devices: 14.9 us -> 6.29 us  [exchange(): return lax.all_to_all(shaped, AXES, split_axis=0, concat_axis=0, tiled=True)]
    pallas_call x2, Pallas kernels: 18.1 us -> 26.7 us  [solve(): pl.pallas_call(functools.partial(solve_kernel, z, f, slots, per_step), gr...]
  transfers between devices with their start and end apart: 18 -> 18, of which waited for: 12 -> 12; matrix products, arithmetic and copies ran while one was open for 0% -> 0% of each run, Pallas kernels for 13% -> 17%
where the time goes in v2:
time: 270 us; the launch traced here: 269 us
  waiting for transfers between devices  161 us (60%)
  Pallas kernels  60.5 us (22%)
  starting transfers between devices  44.9 us (17%)
    ppermute x9, waiting for transfers between devices, swap(): return lax.ppermute(value, axis, [(i, i ^ bit) for i in range(size)])  106 us
    ppermute x4, waiting for transfers between devices, beside(): return (lax.ppermute(last, AXES, up), lax.ppermute(first, AXES, down))  49.1 us
    all_to_all x4, starting transfers between devices, exchange(): return lax.all_to_all(shaped, AXES, split_axis=0, concat_axis=0, tiled=True)  26.9 us
    pallas_call x2, Pallas kernels, solve(): pl.pallas_call(functools.partial(solve_kernel, z, f, slots, per_step), gr...  26.7 us
    pallas_call x2, Pallas kernels, pack(): pl.pallas_call(functools.partial(pack_kernel, z), grid_spec=pltpu.Prefetc...  15.6 us
    ppermute x4, starting transfers between devices, beside(): return (lax.ppermute(last, AXES, up), lax.ppermute(first, AXES, down))  12.1 us
    pallas_call x2, Pallas kernels, unpack(): pl.pallas_call(functools.partial(unpack_kernel, z), grid_spec=pltpu.Prefe...  11 us
    all_to_all x4, waiting for transfers between devices, exchange(): return lax.all_to_all(shaped, AXES, split_axis=0, concat_axis=0, tiled=True)  6.29 us
  transfers between devices with their start and end apart: 18, of which 12 were waited for; matrix products, arithmetic and copies ran while one was open for 0% of the time, Pallas kernels for 17%

profile of v2, /device:TPU:15, one launch (start us, length us, event | category | flops | bytes accessed | tf_op | source)
XLA Modules:
  0.0 269.1 jit_solution(5109384545249912752)
XLA Ops:
  0.6 3.7 %plan.1 = (s32[1]{0:T(128)}, s32[544]{0:T(1024)S(1)}, s32[64]{0:T(128)S(1)}) custom-call(s32[64]{0:T(128)} %start_ref.1), custom_call_target="tpu_custom_call" | custom-call | tf_op jit(solution)/shard_map/plan/pallas_call | solution.py:149
  5.0 263.9 %conditional.1 = (bf16[2,16,544,128]{3,2,1,0:T(8,128)(2,1)}, bf16[2,16,544,128]{3,2,1,0:T(8,128)(2,1)}) conditional(s32[]{:T(128)} %bitcast.30, (s32[544]{0:T(1024)S(1)}, s32[64]{0:T(128)S(1)}, bf16[2,16,544,128]{3,2,1,0:T(8,128)(2,1)}, bf16[2,2,512,512]{3,2,1,0:T(8,128)(2,1)}, s32[64]{0:T(128)}, ...), branch_computations={%region_0.0_spmd, %region_1.0_spmd, %region_2.0_spmd, %region_3.0_... | conditional | flops 24000000000 | bytes 150310416 | solution.py:489
  5.0 5.2 %pack_0.6 = bf16[576,16,128]{2,1,0:T(8,128)(2,1)} custom-call(s32[544]{0:T(1024)S(1)} %get-tuple-element.90.place_ref, s32[64]{0:T(128)S(1)} %get-tuple-element.91.mate_ref, bf16[2,16,544,128]{3,2,1,0:T(8,128)(2,1)} %get-tuple-element.235.field_ref), custom_call_target="tpu_custom_call" | custom-call | flops 1000000000 | bytes 10000000 | tf_op jit(solution)/shard_map/cond/branch_1_fun/pack_0/pallas_call | solution.py:247
  10.3 6.3 %all-to-all-start.6 = ((bf16[32,18,16,128]{3,2,1,0:T(8,128)(2,1)}), bf16[32,18,16,128]{3,2,1,0:T(8,128)(2,1)}, u32[]{:S(2)}, u32[]{:S(2)}) async-start(bf16[32,18,16,128]{3,2,1,0:T(8,128)(2,1)} %bitcast.10), calls=%async_computation.6 | async-start | bytes 4718592 | tf_op jit(solution)/shard_map/cond/branch_1_fun/all_to_all | solution.py:475
  16.6 0.0 copy-done.1
  16.6 0.1 slice_bitcast_fusion.1.rest_0_
  16.7 0.7 collective-permute-start.16
  17.5 0.3 collective-permute-start.15
  17.8 0.3 collective-permute-start.14
  18.1 10.3 %pack_1.6 = (bf16[576,16,128]{2,1,0:T(8,128)(2,1)}, s32[768]{0:T(1024)S(1)}) custom-call(s32[544]{0:T(1024)S(1)} %get-tuple-element.90.place_ref, s32[64]{0:T(128)S(1)} %get-tuple-element.91.mate_ref, bf16[2,16,544,128]{3,2,1,0:T(8,128)(2,1)} %get-tuple-element.235.field_ref), custom_call_target="tpu_custom_call" | custom-call | flops 1000000000 | bytes 10000000 | tf_op jit(solution)/shard_map/cond/branch_1_fun/pack_1/pallas_call | solution.py:247
  28.4 0.0 collective-permute-done.16.rest_8_
  28.4 37.6 %collective-permute-done.15.rest_2_ = bf16[2,512,512]{2,1,0:T(8,128)(2,1)S(1)} collective-permute-done((bf16[2,512,512]{2,1,0:T(8,128)(2,1)S(1)}, bf16[2,512,512]{2,1,0:T(8,128)(2,1)S(1)}, u32[]{:S(2)}, u32[]{:S(2)}) %collective-permute-start.15) | collective-permute-done | bytes 1048608 | tf_op jit(solution)/shard_map/cond/branch_1_fun/ppermute | solution.py:172
  66.0 0.0 collective-permute-done.14.rest_1_
  66.0 2.6 all-to-all-done.6.columns_ref
  68.6 6.9 %all-to-all-start.4 = ((bf16[32,18,16,128]{3,2,1,0:T(8,128)(2,1)}), bf16[32,18,16,128]{3,2,1,0:T(8,128)(2,1)}, u32[]{:S(2)}, u32[]{:S(2)}) async-start(bf16[32,18,16,128]{3,2,1,0:T(8,128)(2,1)} %bitcast.8), calls=%async_computation.4 | async-start | bytes 4718592 | tf_op jit(solution)/shard_map/cond/branch_1_fun/all_to_all | solution.py:475
  75.5 0.3 collective-permute-start.22
  75.9 0.6 collective-permute-start.19
  76.5 0.0 collective-permute-start.18
  76.5 0.5 collective-permute-start.20
  77.0 32.6 %collective-permute-done.22.rest_3_ = bf16[1,512,512]{2,1,0:T(8,128)(2,1)} collective-permute-done((bf16[1,512,512]{2,1,0:T(8,128)(2,1)S(1)}, bf16[1,512,512]{2,1,0:T(8,128)(2,1)}, u32[]{:S(2)}, u32[]{:S(2)}) %collective-permute-start.22) | collective-permute-done | bytes 524320 | tf_op jit(solution)/shard_map/cond/branch_1_fun/ppermute | solution.py:172
  109.7 0.4 collective-permute-start.23
  110.1 1.9 collective-permute-done.23.rest_7_
  112.0 0.0 collective-permute-done.18.rest_4_
  112.0 0.0 collective-permute-done.19.rest_5_
  112.0 0.0 collective-permute-done.20.rest_6_
  112.0 13.5 %solve_0.6 = bf16[32,18,16,128]{3,2,1,0:T(8,128)(2,1)} custom-call(s32[768]{0:T(1024)S(1)} %get-tuple-element.93.holder_ref, s32[64]{0:T(128)S(1)} %copy-done.11, s32[64]{0:T(128)S(1)} %get-tuple-element.91.mate_ref, s32[1]{0:T(128)} %bitcast.6.me_ref, bf16[32,18,16,128]{3,2,1,0:T(8,128)(2,1)} %all-to-all-done.6.columns_ref, ...), custom_call_target="tpu_custom_call" | custom-call | flops 10000000000 | bytes 10000000 | tf_op jit(solution)/shard_map/cond/branch_1_fun/solve_0/pallas_call | solution.py:342
  125.5 1.7 all-to-all-done.4.columns_ref
  127.2 6.9 %all-to-all-start.7 = ((bf16[32,18,16,128]{3,2,1,0:T(8,128)(2,1)}), bf16[32,18,16,128]{3,2,1,0:T(8,128)(2,1)}, u32[]{:S(2)}, u32[]{:S(2)}) async-start(bf16[32,18,16,128]{3,2,1,0:T(8,128)(2,1)} %solve_0.6), calls=%async_computation.7 | async-start | bytes 4718592 | tf_op jit(solution)/shard_map/cond/branch_1_fun/all_to_all | solution.py:475
  134.2 0.3 collective-permute-start.17
  134.5 32.3 %collective-permute-done.17.rest_3_ = bf16[1,512,512]{2,1,0:T(8,128)(2,1)S(1)} collective-permute-done((bf16[1,512,512]{2,1,0:T(8,128)(2,1)S(1)}, bf16[1,512,512]{2,1,0:T(8,128)(2,1)S(1)}, u32[]{:S(2)}, u32[]{:S(2)}) %collective-permute-start.17) | collective-permute-done | bytes 524320 | tf_op jit(solution)/shard_map/cond/branch_1_fun/ppermute | solution.py:172
  166.8 2.3 collective-permute-start.21
  169.1 1.5 collective-permute-done.21.rest_7_
  170.6 13.2 %solve_1.6 = bf16[32,18,16,128]{3,2,1,0:T(8,128)(2,1)} custom-call(s32[768]{0:T(1024)S(1)} %get-tuple-element.93.holder_ref, s32[64]{0:T(128)S(1)} %copy-done.11, s32[64]{0:T(128)S(1)} %get-tuple-element.91.mate_ref, s32[1]{0:T(128)} %bitcast.6.me_ref, bf16[32,18,16,128]{3,2,1,0:T(8,128)(2,1)} %all-to-all-done.4.columns_ref, ...), custom_call_target="tpu_custom_call" | custom-call | flops 10000000000 | bytes 10000000 | tf_op jit(solution)/shard_map/cond/branch_1_fun/solve_1/pallas_call | solution.py:342
  183.9 2.0 all-to-all-done.7
  185.9 6.8 %all-to-all-start.5 = ((bf16[32,18,16,128]{3,2,1,0:T(8,128)(2,1)}), bf16[32,18,16,128]{3,2,1,0:T(8,128)(2,1)S(1)}, u32[]{:S(2)}, u32[]{:S(2)}) async-start(bf16[32,18,16,128]{3,2,1,0:T(8,128)(2,1)} %solve_1.6), calls=%async_computation.5 | async-start | bytes 4718592 | tf_op jit(solution)/shard_map/cond/branch_1_fun/all_to_all | solution.py:475
  192.7 6.4 %unpack_0.6 = (bf16[2,16,544,128]{3,2,1,0:T(8,128)(2,1)}, bf16[2,16,544,128]{3,2,1,0:T(8,128)(2,1)}, bf16[1,544,128]{2,1,0:T(8,128)(2,1)}, bf16[1,544,128]{2,1,0:T(8,128)(2,1)}) custom-call(s32[544]{0:T(1024)S(1)} %get-tuple-element.90.place_ref, s32[64]{0:T(128)S(1)} %get-tuple-element.91.mate_ref, bf16[576,16,128]{2,1,0:T(8,128)(2,1)} %bitcast.11.returned_ref), custom_call_target="tpu_custom_call" | custom-call | flops 1000000000 | bytes 10000000 | tf_op jit(solution)/shard_map/cond/branch_1_fun/unpack_0/pallas_call | solution.py:407
  199.1 3.3 %collective-permute-start.24 = (bf16[1,544,128]{2,1,0:T(8,128)(2,1)}, bf16[1,544,128]{2,1,0:T(8,128)(2,1)S(1)}, u32[]{:S(2)}, u32[]{:S(2)}) collective-permute-start(bf16[1,544,128]{2,1,0:T(8,128)(2,1)} %get-tuple-element.113), channel_id=1, source_target_pairs={{0,1},{1,2},{2,3},{3,4},{4,5},{5,6},{6,7},{7,8},{8,9},{9,10},{10,1... | collective-permute-start | bytes 417800 | tf_op jit(solution)/shard_map/cond/branch_1_fun/ppermute | solution.py:470
  202.4 1.9 collective-permute-start.25
  204.4 41.7 %collective-permute-done.24.before_ref = bf16[1,544,128]{2,1,0:T(8,128)(2,1)S(1)} collective-permute-done((bf16[1,544,128]{2,1,0:T(8,128)(2,1)}, bf16[1,544,128]{2,1,0:T(8,128)(2,1)S(1)}, u32[]{:S(2)}, u32[]{:S(2)}) %collective-permute-start.24) | collective-permute-done | bytes 139296 | tf_op jit(solution)/shard_map/cond/branch_1_fun/ppermute | solution.py:470
  246.1 1.1 collective-permute-done.25.after_ref
  247.2 1.7 edges_0.6.rest_1_
  249.0 0.0 all-to-all-done.5
  249.0 4.6 %unpack_1.6 = (bf16[2,16,544,128]{3,2,1,0:T(8,128)(2,1)}, bf16[2,16,544,128]{3,2,1,0:T(8,128)(2,1)}, bf16[1,544,128]{2,1,0:T(8,128)(2,1)S(1)}, bf16[1,544,128]{2,1,0:T(8,128)(2,1)S(1)}) custom-call(s32[544]{0:T(1024)S(1)} %get-tuple-element.90.place_ref, s32[64]{0:T(128)S(1)} %get-tuple-element.91.mate_ref, ...), custom_call_target="tpu_custom_call", output_to_operand_aliasing={{0}: (3, {}), {1}: (4, {})} | custom-call | flops 1000000000 | bytes 10000000 | tf_op jit(solution)/shard_map/cond/branch_1_fun/unpack_1/pallas_call | solution.py:407
  253.6 4.9 %collective-permute-start.26 = (bf16[1,544,128]{2,1,0:T(8,128)(2,1)S(1)}, bf16[1,544,128]{2,1,0:T(8,128)(2,1)S(1)}, u32[]{:S(2)}, u32[]{:S(2)}) collective-permute-start(bf16[1,544,128]{2,1,0:T(8,128)(2,1)S(1)} %get-tuple-element.117), channel_id=1, source_target_pairs={{0,1},{1,2},{2,3},{3,4},{4,5},{5,6},{6,7},{7,8},{8,9},{9,10},{10,1... | collective-permute-start | bytes 417800 | tf_op jit(solution)/shard_map/cond/branch_1_fun/ppermute | solution.py:470
  258.5 1.9 collective-permute-start.27
  260.5 0.1 collective-permute-done.26.before_ref
  260.6 6.2 %collective-permute-done.27.after_ref = bf16[1,544,128]{2,1,0:T(8,128)(2,1)S(1)} collective-permute-done((bf16[1,544,128]{2,1,0:T(8,128)(2,1)S(1)}, bf16[1,544,128]{2,1,0:T(8,128)(2,1)S(1)}, u32[]{:S(2)}, u32[]{:S(2)}) %collective-permute-start.27) | collective-permute-done | bytes 139296 | tf_op jit(solution)/shard_map/cond/branch_1_fun/ppermute | solution.py:470
  266.7 1.7 edges_1.6
  (7 shorter events, 0.1 us)
Async XLA Ops:
  10.3 6.3 %copy-start.1 = (bf16[2,2,512,512]{3,2,1,0:T(8,128)(2,1)S(1)}, bf16[2,2,512,512]{3,2,1,0:T(8,128)(2,1)}, u32[]{:S(2)}) copy-start(bf16[2,2,512,512]{3,2,1,0:T(8,128)(2,1)} %get-tuple-element.275.inverses_ref) | copy-start | bytes 6291460 | tf_op jit(solution)/shard_map/cond
  10.3 58.3 %all-to-all-start.6 = ((bf16[32,18,16,128]{3,2,1,0:T(8,128)(2,1)}), bf16[32,18,16,128]{3,2,1,0:T(8,128)(2,1)}, u32[]{:S(2)}, u32[]{:S(2)}) async-start(bf16[32,18,16,128]{3,2,1,0:T(8,128)(2,1)} %bitcast.10), calls=%async_computation.6 | async-start | bytes 4718592 | tf_op jit(solution)/shard_map/cond/branch_1_fun/all_to_all | solution.py:475
  16.7 11.7 %collective-permute-start.16 = (bf16[2,512,512]{2,1,0:T(8,128)(2,1)S(1)}, bf16[2,512,512]{2,1,0:T(8,128)(2,1)S(1)}, u32[]{:S(2)}, u32[]{:S(2)}) collective-permute-start(bf16[2,512,512]{2,1,0:T(8,128)(2,1)S(1)} %slice_bitcast_fusion.1.rest_0_), channel_id=1, source_target_pairs={{0,8},{2,10},{4,12},{6,14},{8,0},{10,2},{12,4},{14,6},{16,24},{18,... | collective-permute-start | bytes 3145736 | tf_op jit(solution)/shard_map/cond/branch_1_fun/ppermute | solution.py:179
  17.5 48.6 %collective-permute-start.15 = (bf16[2,512,512]{2,1,0:T(8,128)(2,1)S(1)}, bf16[2,512,512]{2,1,0:T(8,128)(2,1)S(1)}, u32[]{:S(2)}, u32[]{:S(2)}) collective-permute-start(bf16[2,512,512]{2,1,0:T(8,128)(2,1)S(1)} %slice_bitcast_fusion.1.rest_0_), channel_id=1, source_target_pairs={{0,4},{4,0},{8,12},{12,8},{16,20},{20,16},{24,28},{28,24},{1,5},{5... | collective-permute-start | bytes 3145736 | tf_op jit(solution)/shard_map/cond/branch_1_fun/ppermute | solution.py:172
  17.8 48.2 %collective-permute-start.14 = (bf16[2,512,512]{2,1,0:T(8,128)(2,1)S(1)}, bf16[2,512,512]{2,1,0:T(8,128)(2,1)S(1)}, u32[]{:S(2)}, u32[]{:S(2)}) collective-permute-start(bf16[2,512,512]{2,1,0:T(8,128)(2,1)S(1)} %slice_bitcast_fusion.1.rest_0_), channel_id=1, source_target_pairs={{0,2},{1,3},{2,0},{3,1},{4,6},{5,7},{6,4},{7,5},{8,10},{9,11},{10,... | collective-permute-start | bytes 3145736 | tf_op jit(solution)/shard_map/cond/branch_1_fun/ppermute | solution.py:172
  28.4 37.6 %copy-start.6 = (bf16[2,512,512]{2,1,0:T(8,128)(2,1)}, bf16[2,512,512]{2,1,0:T(8,128)(2,1)S(1)}, u32[]{:S(2)}) copy-start(bf16[2,512,512]{2,1,0:T(8,128)(2,1)S(1)} %collective-permute-done.16.rest_8_) | copy-start | bytes 3145732 | tf_op jit(solution)/shard_map/cond
  68.6 43.4 %copy-start.11 = (s32[64]{0:T(128)S(1)}, s32[64]{0:T(128)}, u32[]{:S(2)}) copy-start(s32[64]{0:T(128)} %get-tuple-element.94.start_ref) | copy-start | bytes 772 | tf_op jit(solution)/shard_map/cond
  68.6 58.7 %all-to-all-start.4 = ((bf16[32,18,16,128]{3,2,1,0:T(8,128)(2,1)}), bf16[32,18,16,128]{3,2,1,0:T(8,128)(2,1)}, u32[]{:S(2)}, u32[]{:S(2)}) async-start(bf16[32,18,16,128]{3,2,1,0:T(8,128)(2,1)} %bitcast.8), calls=%async_computation.4 | async-start | bytes 4718592 | tf_op jit(solution)/shard_map/cond/branch_1_fun/all_to_all | solution.py:475
  75.5 34.1 %collective-permute-start.22 = (bf16[1,512,512]{2,1,0:T(8,128)(2,1)S(1)}, bf16[1,512,512]{2,1,0:T(8,128)(2,1)}, u32[]{:S(2)}, u32[]{:S(2)}) collective-permute-start(bf16[1,512,512]{2,1,0:T(8,128)(2,1)S(1)} %slice.35), channel_id=1, source_target_pairs={{0,4},{4,0},{8,12},{12,8},{16,20},{20,16},{24,28},{28,24},{1,5},{5... | collective-permute-start | bytes 1572872 | tf_op jit(solution)/shard_map/cond/branch_1_fun/ppermute | solution.py:172
  75.9 36.1 %collective-permute-start.19 = (bf16[2,512,512]{2,1,0:T(8,128)(2,1)S(1)}, bf16[2,512,512]{2,1,0:T(8,128)(2,1)}, u32[]{:S(2)}, u32[]{:S(2)}) collective-permute-start(bf16[2,512,512]{2,1,0:T(8,128)(2,1)S(1)} %collective-permute-done.14.rest_1_), channel_id=1, source_target_pairs={{0,1},{1,0},{2,3},{3,2},{4,5},{5,4},{6,7},{7,6},{8,9},{9,8},{10,11... | collective-permute-start | bytes 3145736 | tf_op jit(solution)/shard_map/cond/branch_1_fun/ppermute | solution.py:172
  76.5 35.5 %collective-permute-start.18 = (bf16[2,512,512]{2,1,0:T(8,128)(2,1)S(1)}, bf16[2,512,512]{2,1,0:T(8,128)(2,1)}, u32[]{:S(2)}, u32[]{:S(2)}) collective-permute-start(bf16[2,512,512]{2,1,0:T(8,128)(2,1)S(1)} %slice_bitcast_fusion.1.rest_0_), channel_id=1, source_target_pairs={{0,1},{1,0},{2,3},{3,2},{4,5},{5,4},{6,7},{7,6},{8,9},{9,8},{10,11... | collective-permute-start | bytes 3145736 | tf_op jit(solution)/shard_map/cond/branch_1_fun/ppermute | solution.py:172
  76.5 35.5 %collective-permute-start.20 = (bf16[2,512,512]{2,1,0:T(8,128)(2,1)S(1)}, bf16[2,512,512]{2,1,0:T(8,128)(2,1)}, u32[]{:S(2)}, u32[]{:S(2)}) collective-permute-start(bf16[2,512,512]{2,1,0:T(8,128)(2,1)S(1)} %collective-permute-done.15.rest_2_), channel_id=1, source_target_pairs={{0,1},{1,0},{2,3},{3,2},{4,5},{5,4},{6,7},{7,6},{8,9},{9,8},{10,11... | collective-permute-start | bytes 3145736 | tf_op jit(solution)/shard_map/cond/branch_1_fun/ppermute | solution.py:172
  109.7 2.3 collective-permute-start.23
  127.2 58.7 %all-to-all-start.7 = ((bf16[32,18,16,128]{3,2,1,0:T(8,128)(2,1)}), bf16[32,18,16,128]{3,2,1,0:T(8,128)(2,1)}, u32[]{:S(2)}, u32[]{:S(2)}) async-start(bf16[32,18,16,128]{3,2,1,0:T(8,128)(2,1)} %solve_0.6), calls=%async_computation.7 | async-start | bytes 4718592 | tf_op jit(solution)/shard_map/cond/branch_1_fun/all_to_all | solution.py:475
  134.2 32.7 %collective-permute-start.17 = (bf16[1,512,512]{2,1,0:T(8,128)(2,1)S(1)}, bf16[1,512,512]{2,1,0:T(8,128)(2,1)S(1)}, u32[]{:S(2)}, u32[]{:S(2)}) collective-permute-start(bf16[1,512,512]{2,1,0:T(8,128)(2,1)S(1)} %slice.34), channel_id=1, source_target_pairs={{0,2},{1,3},{2,0},{3,1},{4,6},{5,7},{6,4},{7,5},{8,10},{9,11},{10,... | collective-permute-start | bytes 1572872 | tf_op jit(solution)/shard_map/cond/branch_1_fun/ppermute | solution.py:172
  166.8 3.8 %collective-permute-start.21 = (bf16[1,512,512]{2,1,0:T(8,128)(2,1)S(1)}, bf16[1,512,512]{2,1,0:T(8,128)(2,1)S(1)}, u32[]{:S(2)}, u32[]{:S(2)}) collective-permute-start(bf16[1,512,512]{2,1,0:T(8,128)(2,1)S(1)} %collective-permute-done.17.rest_3_), channel_id=1, source_target_pairs={{0,1},{1,0},{2,3},{3,2},{4,5},{5,4},{6,7},{7,6},{8,9},{9,8},{10,11... | collective-permute-start | bytes 1572872 | tf_op jit(solution)/shard_map/cond/branch_1_fun/ppermute | solution.py:172
  185.9 63.1 %all-to-all-start.5 = ((bf16[32,18,16,128]{3,2,1,0:T(8,128)(2,1)}), bf16[32,18,16,128]{3,2,1,0:T(8,128)(2,1)S(1)}, u32[]{:S(2)}, u32[]{:S(2)}) async-start(bf16[32,18,16,128]{3,2,1,0:T(8,128)(2,1)} %solve_1.6), calls=%async_computation.5 | async-start | bytes 4718592 | tf_op jit(solution)/shard_map/cond/branch_1_fun/all_to_all | solution.py:475
  199.1 47.0 %collective-permute-start.24 = (bf16[1,544,128]{2,1,0:T(8,128)(2,1)}, bf16[1,544,128]{2,1,0:T(8,128)(2,1)S(1)}, u32[]{:S(2)}, u32[]{:S(2)}) collective-permute-start(bf16[1,544,128]{2,1,0:T(8,128)(2,1)} %get-tuple-element.113), channel_id=1, source_target_pairs={{0,1},{1,2},{2,3},{3,4},{4,5},{5,6},{6,7},{7,8},{8,9},{9,10},{10,1... | collective-permute-start | bytes 417800 | tf_op jit(solution)/shard_map/cond/branch_1_fun/ppermute | solution.py:470
  202.4 44.8 %collective-permute-start.25 = (bf16[1,544,128]{2,1,0:T(8,128)(2,1)}, bf16[1,544,128]{2,1,0:T(8,128)(2,1)S(1)}, u32[]{:S(2)}, u32[]{:S(2)}) collective-permute-start(bf16[1,544,128]{2,1,0:T(8,128)(2,1)} %get-tuple-element.114), channel_id=1, source_target_pairs={{1,0},{2,1},{3,2},{4,3},{5,4},{6,5},{7,6},{8,7},{9,8},{10,9},{11,1... | collective-permute-start | bytes 417800 | tf_op jit(solution)/shard_map/cond/branch_1_fun/ppermute | solution.py:470
  253.6 6.9 %collective-permute-start.26 = (bf16[1,544,128]{2,1,0:T(8,128)(2,1)S(1)}, bf16[1,544,128]{2,1,0:T(8,128)(2,1)S(1)}, u32[]{:S(2)}, u32[]{:S(2)}) collective-permute-start(bf16[1,544,128]{2,1,0:T(8,128)(2,1)S(1)} %get-tuple-element.117), channel_id=1, source_target_pairs={{0,1},{1,2},{2,3},{3,4},{4,5},{5,6},{6,7},{7,8},{8,9},{9,10},{10,1... | collective-permute-start | bytes 417800 | tf_op jit(solution)/shard_map/cond/branch_1_fun/ppermute | solution.py:470
  258.5 8.2 %collective-permute-start.27 = (bf16[1,544,128]{2,1,0:T(8,128)(2,1)S(1)}, bf16[1,544,128]{2,1,0:T(8,128)(2,1)S(1)}, u32[]{:S(2)}, u32[]{:S(2)}) collective-permute-start(bf16[1,544,128]{2,1,0:T(8,128)(2,1)S(1)} %get-tuple-element.118), channel_id=1, source_target_pairs={{1,0},{2,1},{3,2},{4,3},{5,4},{6,5},{7,6},{8,7},{9,8},{10,9},{11,1... | collective-permute-start | bytes 417800 | tf_op jit(solution)/shard_map/cond/branch_1_fun/ppermute | solution.py:470

commit v3 on v2

--- a/solution.py
+++ b/solution.py
@@ -15,6 +15,7 @@
 GIFT = 8
 GROUP = 16
 VMEM = 48 << 20
+MORE_VMEM = 60 << 20
 RIDES = 8
 
 inner_radius = 0.35
@@ -358,7 +359,7 @@
 
 
 def unpack_kernel(z, place_ref, mate_ref, returned_ref, *rest):
-    grid_ref, slope_ref, first_ref, last_ref, wide_ref = rest[-5:]
+    grid_ref, slope_ref, wide_ref = rest[-3:]
     pitch = z.blocks + 1
 
     def gather(g, carry):
@@ -392,8 +393,6 @@
         for i in range(1, z.local - 1):
             slope = 0.5 * (value[i + 1] - value[i - 1])
             slope_ref[0, i, rows, :] = slope.astype(jnp.bfloat16)
-        first_ref[0, rows, :] = value[0].astype(jnp.bfloat16)
-        last_ref[0, rows, :] = value[-1].astype(jnp.bfloat16)
         return carry
 
     lax.fori_loop(0, z.blocks // GROUP, group, 0, unroll=2)
@@ -401,9 +400,7 @@
 
 def unpack(z, place, mate, returned, f, earlier):
     whole = jax.ShapeDtypeStruct((z.fields, z.local, z.blocks, z.width), jnp.bfloat16)
-    level = jax.ShapeDtypeStruct((1, z.blocks, z.width), jnp.bfloat16)
     spec = pl.BlockSpec((1, z.local, z.blocks, z.width), lambda i, *s: (f, 0, 0, 0))
-    level_spec = pl.BlockSpec(level.shape, lambda i, *s: (0, 0, 0))
     return pl.pallas_call(
         functools.partial(unpack_kernel, z),
         grid_spec=pltpu.PrefetchScalarGridSpec(
@@ -411,57 +408,103 @@
             grid=(1,),
             in_specs=[pl.BlockSpec(returned.shape, lambda i, *s: (0, 0, 0))]
             + [pl.BlockSpec(memory_space=pl.ANY)] * len(earlier),
-            out_specs=[spec, spec, level_spec, level_spec],
+            out_specs=[spec, spec],
             scratch_shapes=[pltpu.VMEM((z.local * (z.blocks + 1), z.width), jnp.float32)],
         ),
-        out_shape=[whole, whole, level, level],
+        out_shape=[whole, whole],
         input_output_aliases={3 + i: i for i in range(len(earlier))},
-        compiler_params=pltpu.CompilerParams(vmem_limit_bytes=VMEM if earlier else 60 << 20),
+        compiler_params=pltpu.CompilerParams(vmem_limit_bytes=VMEM if earlier else MORE_VMEM),
         cost_estimate=pl.CostEstimate(flops=10**9, bytes_accessed=10**7, transcendentals=0),
         name=f"unpack_{f}",
     )(place, mate, returned, *earlier)
 
 
-def edge_kernel(z, f, second_ref, before_last_ref, before_ref, after_ref, slope_in_ref, slope_ref,
-                edge_ref, sems):
-    del slope_in_ref
-
-    def wide(ref):
-        return ref[...].reshape(z.blocks, z.width).astype(jnp.float32)
-
-    slopes = [wide(second_ref) - wide(before_ref), wide(after_ref) - wide(before_last_ref)]
+def rim_kernel(z, place_ref, mate_ref, returned_ref, first_ref, last_ref, first_wide_ref, last_wide_ref):
+    sides = ((first_wide_ref, 0), (last_wide_ref, z.local - 1))
+
+    def gather(g, carry):
+        for k in range(GROUP):
+            b = g * GROUP + k
+            tile = returned_ref[place_ref[b]].astype(jnp.float32)
+            for wide_ref, row in sides:
+                wide_ref[pl.ds(b, 1), :] = tile[row : row + 1]
+        return carry
+
+    lax.fori_loop(0, z.blocks // GROUP, gather, 0)
+    column = lax.broadcasted_iota(jnp.int32, (z.local, z.width), 1)
+
+    def ride(q, carry):
+        b, host_block, live = riding(z, mate_ref, q)
+        tile = returned_ref[place_ref[b]].astype(jnp.float32)
+        rider = pltpu.roll(tile, z.width - live, 1)
+        rider = jnp.where(column < z.last_live(q), rider, 0.0)
+        tile = jnp.where(column < live, tile, 0.0)
+        for wide_ref, row in sides:
+            wide_ref[pl.ds(host_block, 1), :] = tile[row : row + 1]
+            wide_ref[pl.ds(b, 1), :] = rider[row : row + 1]
+        return carry
+
+    lax.fori_loop(z.degrees // 2, z.degrees, ride, 0, unroll=RIDES)
+    first_ref[0] = first_wide_ref[...].astype(jnp.bfloat16)
+    last_ref[0] = last_wide_ref[...].astype(jnp.bfloat16)
+
+
+def rims(z, place, mate, returned, f):
+    level = jax.ShapeDtypeStruct((1, z.blocks, z.width), jnp.bfloat16)
+    spec = pl.BlockSpec(level.shape, lambda i, *s: (0, 0, 0))
+    return pl.pallas_call(
+        functools.partial(rim_kernel, z),
+        grid_spec=pltpu.PrefetchScalarGridSpec(
+            num_scalar_prefetch=2,
+            grid=(1,),
+            in_specs=[pl.BlockSpec(returned.shape, lambda i, *s: (0, 0, 0))],
+            out_specs=[spec, spec],
+            scratch_shapes=[pltpu.VMEM((z.blocks, z.width), jnp.float32)] * 2,
+        ),
+        out_shape=[level, level],
+        compiler_params=pltpu.CompilerParams(vmem_limit_bytes=VMEM if f else MORE_VMEM),
+        cost_estimate=pl.CostEstimate(flops=10**8, bytes_accessed=3 * 10**6, transcendentals=0),
+        name=f"rims_{f}",
+    )(place, mate, returned)
+
+
+def edge_kernel(z, *refs):
+    count = 4 * z.fields
+    inner, outer, (_, slope_ref, edge_ref, sems) = refs[: count // 2], refs[count // 2 : count], refs[count:]
     copies = []
-    for i, level in enumerate((0, z.local - 1)):
-        edge_ref[i] = (0.5 * slopes[i]).astype(jnp.bfloat16)
-        copies.append(pltpu.make_async_copy(edge_ref.at[i], slope_ref.at[f, level], sems.at[i]))
+    for i in range(2 * z.fields):
+        inside = inner[i][...].reshape(z.blocks, z.width).astype(jnp.float32)
+        outside = outer[i][...].reshape(z.blocks, z.width).astype(jnp.float32)
+        slope = inside - outside if i % 2 == 0 else outside - inside
+        edge_ref[i] = (0.5 * slope).astype(jnp.bfloat16)
+        level = i % 2 * (z.local - 1)
+        copies.append(pltpu.make_async_copy(edge_ref.at[i], slope_ref.at[i // 2, level], sems.at[i]))
         copies[i].start()
     for copy in copies:
         copy.wait()
 
 
-def edges(z, slope, grid, before, after, f):
-    block = (1, 1, z.blocks, z.width)
-    beside_spec = pl.BlockSpec((1, z.blocks, z.width), lambda i: (0, 0, 0))
+def edges(z, slope, grid, outside):
+    def inner(f, level):
+        return pl.BlockSpec((1, 1, z.blocks, z.width), lambda i: (f, level, 0, 0))
+
+    inner_specs = [inner(f, level) for f in range(z.fields) for level in (1, z.local - 2)]
+    outer_spec = pl.BlockSpec((1, z.blocks, z.width), lambda i: (0, 0, 0))
+    count = len(inner_specs)
     return pl.pallas_call(
-        functools.partial(edge_kernel, z, f),
+        functools.partial(edge_kernel, z),
         grid=(1,),
-        in_specs=[
-            pl.BlockSpec(block, lambda i: (f, 1, 0, 0)),
-            pl.BlockSpec(block, lambda i: (f, z.local - 2, 0, 0)),
-            beside_spec,
-            beside_spec,
-            pl.BlockSpec(memory_space=pl.ANY),
-        ],
+        in_specs=inner_specs + [outer_spec] * count + [pl.BlockSpec(memory_space=pl.ANY)],
         out_specs=pl.BlockSpec(memory_space=pl.ANY),
         out_shape=jax.ShapeDtypeStruct(slope.shape, slope.dtype),
         scratch_shapes=[
-            pltpu.VMEM((2, z.blocks, z.width), jnp.bfloat16),
-            pltpu.SemaphoreType.DMA((2,)),
+            pltpu.VMEM((count, z.blocks, z.width), jnp.bfloat16),
+            pltpu.SemaphoreType.DMA((count,)),
         ],
-        input_output_aliases={4: 0},
+        input_output_aliases={2 * count: 0},
         compiler_params=pltpu.CompilerParams(vmem_limit_bytes=VMEM),
-        name=f"edges_{f}",
-    )(grid, grid, before, after, slope)
+        name="edges",
+    )(*[grid] * count, *outside, slope)
 
 
 def beside(z, first, last):
@@ -509,11 +552,12 @@
         exchange(z, solved[f], slots).reshape(z.devices * slots, z.local, z.width)
         for f in range(z.fields)
     ]
-    outs = ()
-    for f in range(z.fields):
-        grid, slope, first, last = unpack(z, place, mate, returned[f], f, outs)
-        outs = (grid, edges(z, slope, grid, *beside(z, first, last), f))
-    return outs
+    outside = [*beside(z, *rims(z, place, mate, returned[0], 0))]
+    outs = unpack(z, place, mate, returned[0], 0, ())
+    last, *outs = lax.optimization_barrier((returned[1], *outs))
+    outside.extend(beside(z, *rims(z, place, mate, last, 1)))
+    grid, slope = unpack(z, place, mate, last, 1, outs)
+    return grid, edges(z, slope, grid, outside)
 
 
 def plain_body(z, grid_field, inverses, degree_start):

time: 270 us -> 252 us (0.933)
  waiting for transfers between devices: 161 us -> 140 us
  Pallas kernels: 60.5 us -> 65.6 us
  starting transfers between devices: 44.9 us -> 41.7 us
    ppermute x4, waiting for transfers between devices: 49.1 us -> 1.6 us  [beside(): return (lax.ppermute(last, AXES, up), lax.ppermute(first, AXES, down))]
    all_to_all x4, waiting for transfers between devices: 6.29 us -> 34.8 us  [exchange(): return lax.all_to_all(shaped, AXES, split_axis=0, concat_axis=0, tiled=True)]
    pallas_call x2 -> x3, Pallas kernels: 3.48 us -> 8.42 us  [the longest x2 6.44 us: rims(): pl.pallas_call(functools.partial(rim_kernel, z), grid_spec=pltpu.Prefetch...]
  transfers between devices with their start and end apart: 18 -> 18, of which waited for: 12 -> 10; matrix products, arithmetic and copies ran while one was open for 0% -> 0% of each run, Pallas kernels for 17% -> 22%
where the time goes in v3:
time: 252 us; the launch traced here: 250 us
  waiting for transfers between devices  140 us (56%)
  Pallas kernels  65.6 us (26%)
  starting transfers between devices  41.7 us (17%)
    ppermute x9, waiting for transfers between devices, swap(): return lax.ppermute(value, axis, [(i, i ^ bit) for i in range(size)])  104 us
    all_to_all x4, waiting for transfers between devices, exchange(): return lax.all_to_all(shaped, AXES, split_axis=0, concat_axis=0, tiled=True)  34.8 us
    all_to_all x4, starting transfers between devices, exchange(): return lax.all_to_all(shaped, AXES, split_axis=0, concat_axis=0, tiled=True)  26.9 us
    pallas_call x2, Pallas kernels, solve(): pl.pallas_call(functools.partial(solve_kernel, z, f, slots, per_step), gr...  26.6 us
    pallas_call x2, Pallas kernels, pack(): pl.pallas_call(functools.partial(pack_kernel, z), grid_spec=pltpu.Prefetc...  15.5 us
    pallas_call x2, Pallas kernels, unpack(): pl.pallas_call(functools.partial(unpack_kernel, z), grid_spec=pltpu.Prefe...  10.9 us
    ppermute x4, starting transfers between devices, beside(): return (lax.ppermute(last, AXES, up), lax.ppermute(first, AXES, down))  10.3 us
    pallas_call x2, Pallas kernels, rims(): pl.pallas_call(functools.partial(rim_kernel, z), grid_spec=pltpu.Prefetch...  6.44 us
  transfers between devices with their start and end apart: 18, of which 10 were waited for; matrix products, arithmetic and copies ran while one was open for 0% of the time, Pallas kernels for 22%

profile of v3, /device:TPU:15, one launch (start us, length us, event | category | flops | bytes accessed | tf_op | source)
XLA Modules:
  0.0 249.7 jit_solution(14335353720018476491)
XLA Ops:
  0.6 4.1 %plan.1 = (s32[1]{0:T(128)}, s32[544]{0:T(1024)S(1)}, s32[64]{0:T(128)S(1)}) custom-call(s32[64]{0:T(128)} %start_ref.1), custom_call_target="tpu_custom_call" | custom-call | tf_op jit(solution)/shard_map/plan/pallas_call | solution.py:150
  5.4 244.1 %conditional.1 = (bf16[2,16,544,128]{3,2,1,0:T(8,128)(2,1)}, bf16[2,16,544,128]{3,2,1,0:T(8,128)(2,1)}) conditional(s32[]{:T(128)} %bitcast.30, (s32[544]{0:T(1024)S(1)}, s32[64]{0:T(128)S(1)}, bf16[2,16,544,128]{3,2,1,0:T(8,128)(2,1)}, bf16[2,2,512,512]{3,2,1,0:T(8,128)(2,1)}, s32[64]{0:T(128)}, ...), branch_computations={%region_0.0_spmd, %region_1.0_spmd, %region_2.0_spmd, %region_3.0_... | conditional | flops 24199999488 | bytes 156310416 | solution.py:532
  5.4 5.2 %pack_0.5 = bf16[544,16,128]{2,1,0:T(8,128)(2,1)} custom-call(s32[544]{0:T(1024)S(1)} %get-tuple-element.60.place_ref, s32[64]{0:T(128)S(1)} %get-tuple-element.61.mate_ref, bf16[2,16,544,128]{3,2,1,0:T(8,128)(2,1)} %get-tuple-element.249.field_ref), custom_call_target="tpu_custom_call" | custom-call | flops 1000000000 | bytes 10000000 | tf_op jit(solution)/shard_map/cond/branch_0_fun/pack_0/pallas_call | solution.py:248
  10.7 6.3 %all-to-all-start.2 = ((bf16[32,17,16,128]{3,2,1,0:T(8,128)(2,1)}), bf16[32,17,16,128]{3,2,1,0:T(8,128)(2,1)}, u32[]{:S(2)}, u32[]{:S(2)}) async-start(bf16[32,17,16,128]{3,2,1,0:T(8,128)(2,1)} %bitcast.4), calls=%async_computation.2 | async-start | bytes 4456448 | tf_op jit(solution)/shard_map/cond/branch_0_fun/all_to_all | solution.py:518
  17.0 0.1 slice_bitcast_fusion.rest_0_
  17.1 0.7 collective-permute-start.2
  17.8 0.3 collective-permute-start.1
  18.2 0.3 collective-permute-start
  18.4 10.3 %pack_1.5 = (bf16[544,16,128]{2,1,0:T(8,128)(2,1)}, s32[768]{0:T(1024)S(1)}) custom-call(s32[544]{0:T(1024)S(1)} %get-tuple-element.60.place_ref, s32[64]{0:T(128)S(1)} %get-tuple-element.61.mate_ref, bf16[2,16,544,128]{3,2,1,0:T(8,128)(2,1)} %get-tuple-element.249.field_ref), custom_call_target="tpu_custom_call" | custom-call | flops 1000000000 | bytes 10000000 | tf_op jit(solution)/shard_map/cond/branch_0_fun/pack_1/pallas_call | solution.py:248
  28.7 0.0 collective-permute-done.2.rest_8_
  28.8 36.1 %collective-permute-done.1.rest_2_ = bf16[2,512,512]{2,1,0:T(8,128)(2,1)S(1)} collective-permute-done((bf16[2,512,512]{2,1,0:T(8,128)(2,1)S(1)}, bf16[2,512,512]{2,1,0:T(8,128)(2,1)S(1)}, u32[]{:S(2)}, u32[]{:S(2)}) %collective-permute-start.1) | collective-permute-done | bytes 1048608 | tf_op jit(solution)/shard_map/cond/branch_0_fun/ppermute | solution.py:173
  64.9 0.0 collective-permute-done.rest_1_
  64.9 1.3 all-to-all-done.2.columns_ref
  66.1 6.9 %all-to-all-start = ((bf16[32,17,16,128]{3,2,1,0:T(8,128)(2,1)}), bf16[32,17,16,128]{3,2,1,0:T(8,128)(2,1)}, u32[]{:S(2)}, u32[]{:S(2)}) async-start(bf16[32,17,16,128]{3,2,1,0:T(8,128)(2,1)} %bitcast.2), calls=%async_computation | async-start | bytes 4456448 | tf_op jit(solution)/shard_map/cond/branch_0_fun/all_to_all | solution.py:518
  73.1 0.3 collective-permute-start.8
  73.4 0.6 collective-permute-start.5
  74.0 0.0 collective-permute-start.4
  74.0 0.5 collective-permute-start.6
  74.6 31.5 %collective-permute-done.8.rest_3_ = bf16[1,512,512]{2,1,0:T(8,128)(2,1)} collective-permute-done((bf16[1,512,512]{2,1,0:T(8,128)(2,1)S(1)}, bf16[1,512,512]{2,1,0:T(8,128)(2,1)}, u32[]{:S(2)}, u32[]{:S(2)}) %collective-permute-start.8) | collective-permute-done | bytes 524320 | tf_op jit(solution)/shard_map/cond/branch_0_fun/ppermute | solution.py:173
  106.0 0.4 collective-permute-start.9
  106.5 1.9 collective-permute-done.9.rest_7_
  108.3 0.0 collective-permute-done.4.rest_4_
  108.3 0.0 collective-permute-done.5.rest_5_
  108.3 0.0 collective-permute-done.6.rest_6_
  108.4 13.5 %solve_0.5 = bf16[32,17,16,128]{3,2,1,0:T(8,128)(2,1)} custom-call(s32[768]{0:T(1024)S(1)} %get-tuple-element.63.holder_ref, s32[64]{0:T(128)S(1)} %copy-done.10, s32[64]{0:T(128)S(1)} %get-tuple-element.61.mate_ref, s32[1]{0:T(128)} %bitcast.me_ref, bf16[32,17,16,128]{3,2,1,0:T(8,128)(2,1)} %all-to-all-done.2.columns_ref, ...), custom_call_target="tpu_custom_call" | custom-call | flops 10000000000 | bytes 10000000 | tf_op jit(solution)/shard_map/cond/branch_0_fun/solve_0/pallas_call | solution.py:343
  121.8 0.1 all-to-all-done.columns_ref
  122.0 6.9 %all-to-all-start.3 = ((bf16[32,17,16,128]{3,2,1,0:T(8,128)(2,1)}), bf16[32,17,16,128]{3,2,1,0:T(8,128)(2,1)}, u32[]{:S(2)}, u32[]{:S(2)}) async-start(bf16[32,17,16,128]{3,2,1,0:T(8,128)(2,1)} %solve_0.5), calls=%async_computation.3 | async-start | bytes 4456448 | tf_op jit(solution)/shard_map/cond/branch_0_fun/all_to_all | solution.py:518
  128.9 0.3 collective-permute-start.3
  129.2 32.7 %collective-permute-done.3.rest_3_ = bf16[1,512,512]{2,1,0:T(8,128)(2,1)S(1)} collective-permute-done((bf16[1,512,512]{2,1,0:T(8,128)(2,1)S(1)}, bf16[1,512,512]{2,1,0:T(8,128)(2,1)S(1)}, u32[]{:S(2)}, u32[]{:S(2)}) %collective-permute-start.3) | collective-permute-done | bytes 524320 | tf_op jit(solution)/shard_map/cond/branch_0_fun/ppermute | solution.py:173
  161.9 0.8 collective-permute-start.7
  162.8 1.5 collective-permute-done.7.rest_7_
  164.3 13.2 %solve_1.5 = bf16[32,17,16,128]{3,2,1,0:T(8,128)(2,1)} custom-call(s32[768]{0:T(1024)S(1)} %get-tuple-element.63.holder_ref, s32[64]{0:T(128)S(1)} %copy-done.10, s32[64]{0:T(128)S(1)} %get-tuple-element.61.mate_ref, s32[1]{0:T(128)} %bitcast.me_ref, bf16[32,17,16,128]{3,2,1,0:T(8,128)(2,1)} %all-to-all-done.columns_ref, ...), custom_call_target="tpu_custom_call" | custom-call | flops 10000000000 | bytes 10000000 | tf_op jit(solution)/shard_map/cond/branch_0_fun/solve_1/pallas_call | solution.py:343
  177.5 0.4 all-to-all-done.3
  177.8 6.8 %all-to-all-start.1 = ((bf16[32,17,16,128]{3,2,1,0:T(8,128)(2,1)}), bf16[32,17,16,128]{3,2,1,0:T(8,128)(2,1)S(1)}, u32[]{:S(2)}, u32[]{:S(2)}) async-start(bf16[32,17,16,128]{3,2,1,0:T(8,128)(2,1)} %solve_1.5), calls=%async_computation.1 | async-start | bytes 4456448 | tf_op jit(solution)/shard_map/cond/branch_0_fun/all_to_all | solution.py:518
  184.7 4.4 %rims_0.5 = (bf16[1,544,128]{2,1,0:T(8,128)(2,1)}, bf16[1,544,128]{2,1,0:T(8,128)(2,1)}) custom-call(s32[544]{0:T(1024)S(1)} %get-tuple-element.60.place_ref, s32[64]{0:T(128)S(1)} %get-tuple-element.61.mate_ref, bf16[544,16,128]{2,1,0:T(8,128)(2,1)} %bitcast.5.returned_ref), custom_call_target="tpu_custom_call" | custom-call | flops 100000000 | bytes 3000000 | tf_op jit(solution)/shard_map/cond/branch_0_fun/rims_0/pallas_call | solution.py:455
  189.0 3.3 %collective-permute-start.10 = (bf16[1,544,128]{2,1,0:T(8,128)(2,1)}, bf16[1,544,128]{2,1,0:T(8,128)(2,1)S(1)}, u32[]{:S(2)}, u32[]{:S(2)}) collective-permute-start(bf16[1,544,128]{2,1,0:T(8,128)(2,1)} %get-tuple-element.88), channel_id=1, source_target_pairs={{0,1},{1,2},{2,3},{3,4},{4,5},{5,6},{6,7},{7,8},{8,9},{9,10},{10,1... | collective-permute-start | bytes 417800 | tf_op jit(solution)/shard_map/cond/branch_0_fun/ppermute | solution.py:513
  192.4 1.9 collective-permute-start.11
  194.3 6.3 %unpack_0.5 = (bf16[2,16,544,128]{3,2,1,0:T(8,128)(2,1)}, bf16[2,16,544,128]{3,2,1,0:T(8,128)(2,1)}) custom-call(s32[544]{0:T(1024)S(1)} %get-tuple-element.60.place_ref, s32[64]{0:T(128)S(1)} %get-tuple-element.61.mate_ref, bf16[544,16,128]{2,1,0:T(8,128)(2,1)} %bitcast.5.returned_ref), custom_call_target="tpu_custom_call" | custom-call | flops 1000000000 | bytes 10000000 | tf_op jit(solution)/shard_map/cond/branch_0_fun/unpack_0/pallas_call | solution.py:404
  200.6 33.1 %all-to-all-done.1 = bf16[32,17,16,128]{3,2,1,0:T(8,128)(2,1)S(1)} async-done(((bf16[32,17,16,128]{3,2,1,0:T(8,128)(2,1)}), bf16[32,17,16,128]{3,2,1,0:T(8,128)(2,1)S(1)}, u32[]{:S(2)}, u32[]{:S(2)}) %all-to-all-start.1) | async-done | bytes 2228256 | tf_op jit(solution)/shard_map/cond/branch_0_fun/all_to_all | solution.py:518
  233.7 2.1 rims_1.5
  235.7 3.1 %collective-permute-start.12 = (bf16[1,544,128]{2,1,0:T(8,128)(2,1)S(1)}, bf16[1,544,128]{2,1,0:T(8,128)(2,1)S(1)}, u32[]{:S(2)}, u32[]{:S(2)}) collective-permute-start(bf16[1,544,128]{2,1,0:T(8,128)(2,1)S(1)} %get-tuple-element.90), channel_id=1, source_target_pairs={{0,1},{1,2},{2,3},{3,4},{4,5},{5,6},{6,7},{7,8},{8,9},{9,10},{10,1... | collective-permute-start | bytes 417800 | tf_op jit(solution)/shard_map/cond/branch_0_fun/ppermute | solution.py:513
  238.8 1.9 collective-permute-start.13
  240.7 4.6 %unpack_1.5 = (bf16[2,16,544,128]{3,2,1,0:T(8,128)(2,1)}, bf16[2,16,544,128]{3,2,1,0:T(8,128)(2,1)}) custom-call(s32[544]{0:T(1024)S(1)} %get-tuple-element.60.place_ref, s32[64]{0:T(128)S(1)} %get-tuple-element.61.mate_ref, bf16[544,16,128]{2,1,0:T(8,128)(2,1)S(1)} %bitcast.45, ...), custom_call_target="tpu_custom_call", output_to_operand_aliasing={{0}: (3, {}), {1}: (4, {})} | custom-call | flops 1000000000 | bytes 10000000 | tf_op jit(solution)/shard_map/cond/branch_0_fun/unpack_1/pallas_call | solution.py:404
  245.4 0.0 collective-permute-done.10.refs_4_
  245.4 0.0 collective-permute-done.11.refs_5_
  245.4 0.0 collective-permute-done.12.refs_6_
  245.4 1.6 collective-permute-done.13.refs_7_
  247.0 2.0 edges.5
  (8 shorter events, 0.1 us)
Async XLA Ops:
  10.7 6.3 %copy-start = (bf16[2,2,512,512]{3,2,1,0:T(8,128)(2,1)S(1)}, bf16[2,2,512,512]{3,2,1,0:T(8,128)(2,1)}, u32[]{:S(2)}) copy-start(bf16[2,2,512,512]{3,2,1,0:T(8,128)(2,1)} %get-tuple-element.282.inverses_ref) | copy-start | bytes 6291460 | tf_op jit(solution)/shard_map/cond
  10.7 55.5 %all-to-all-start.2 = ((bf16[32,17,16,128]{3,2,1,0:T(8,128)(2,1)}), bf16[32,17,16,128]{3,2,1,0:T(8,128)(2,1)}, u32[]{:S(2)}, u32[]{:S(2)}) async-start(bf16[32,17,16,128]{3,2,1,0:T(8,128)(2,1)} %bitcast.4), calls=%async_computation.2 | async-start | bytes 4456448 | tf_op jit(solution)/shard_map/cond/branch_0_fun/all_to_all | solution.py:518
  17.1 11.7 %collective-permute-start.2 = (bf16[2,512,512]{2,1,0:T(8,128)(2,1)S(1)}, bf16[2,512,512]{2,1,0:T(8,128)(2,1)S(1)}, u32[]{:S(2)}, u32[]{:S(2)}) collective-permute-start(bf16[2,512,512]{2,1,0:T(8,128)(2,1)S(1)} %slice_bitcast_fusion.rest_0_), channel_id=1, source_target_pairs={{0,8},{2,10},{4,12},{6,14},{8,0},{10,2},{12,4},{14,6},{16,24},{18,... | collective-permute-start | bytes 3145736 | tf_op jit(solution)/shard_map/cond/branch_0_fun/ppermute | solution.py:180
  17.8 47.1 %collective-permute-start.1 = (bf16[2,512,512]{2,1,0:T(8,128)(2,1)S(1)}, bf16[2,512,512]{2,1,0:T(8,128)(2,1)S(1)}, u32[]{:S(2)}, u32[]{:S(2)}) collective-permute-start(bf16[2,512,512]{2,1,0:T(8,128)(2,1)S(1)} %slice_bitcast_fusion.rest_0_), channel_id=1, source_target_pairs={{0,4},{4,0},{8,12},{12,8},{16,20},{20,16},{24,28},{28,24},{1,5},{5... | collective-permute-start | bytes 3145736 | tf_op jit(solution)/shard_map/cond/branch_0_fun/ppermute | solution.py:173
  18.2 46.7 %collective-permute-start = (bf16[2,512,512]{2,1,0:T(8,128)(2,1)S(1)}, bf16[2,512,512]{2,1,0:T(8,128)(2,1)S(1)}, u32[]{:S(2)}, u32[]{:S(2)}) collective-permute-start(bf16[2,512,512]{2,1,0:T(8,128)(2,1)S(1)} %slice_bitcast_fusion.rest_0_), channel_id=1, source_target_pairs={{0,2},{1,3},{2,0},{3,1},{4,6},{5,7},{6,4},{7,5},{8,10},{9,11},{10,... | collective-permute-start | bytes 3145736 | tf_op jit(solution)/shard_map/cond/branch_0_fun/ppermute | solution.py:173
  28.7 36.1 %copy-start.5 = (bf16[2,512,512]{2,1,0:T(8,128)(2,1)}, bf16[2,512,512]{2,1,0:T(8,128)(2,1)S(1)}, u32[]{:S(2)}) copy-start(bf16[2,512,512]{2,1,0:T(8,128)(2,1)S(1)} %collective-permute-done.2.rest_8_) | copy-start | bytes 3145732 | tf_op jit(solution)/shard_map/cond
  66.1 42.2 %copy-start.10 = (s32[64]{0:T(128)S(1)}, s32[64]{0:T(128)}, u32[]{:S(2)}) copy-start(s32[64]{0:T(128)} %get-tuple-element.64.start_ref) | copy-start | bytes 772 | tf_op jit(solution)/shard_map/cond
  66.1 55.8 %all-to-all-start = ((bf16[32,17,16,128]{3,2,1,0:T(8,128)(2,1)}), bf16[32,17,16,128]{3,2,1,0:T(8,128)(2,1)}, u32[]{:S(2)}, u32[]{:S(2)}) async-start(bf16[32,17,16,128]{3,2,1,0:T(8,128)(2,1)} %bitcast.2), calls=%async_computation | async-start | bytes 4456448 | tf_op jit(solution)/shard_map/cond/branch_0_fun/all_to_all | solution.py:518
  73.1 33.0 %collective-permute-start.8 = (bf16[1,512,512]{2,1,0:T(8,128)(2,1)S(1)}, bf16[1,512,512]{2,1,0:T(8,128)(2,1)}, u32[]{:S(2)}, u32[]{:S(2)}) collective-permute-start(bf16[1,512,512]{2,1,0:T(8,128)(2,1)S(1)} %slice.32), channel_id=1, source_target_pairs={{0,4},{4,0},{8,12},{12,8},{16,20},{20,16},{24,28},{28,24},{1,5},{5... | collective-permute-start | bytes 1572872 | tf_op jit(solution)/shard_map/cond/branch_0_fun/ppermute | solution.py:173
  73.4 34.9 %collective-permute-start.5 = (bf16[2,512,512]{2,1,0:T(8,128)(2,1)S(1)}, bf16[2,512,512]{2,1,0:T(8,128)(2,1)}, u32[]{:S(2)}, u32[]{:S(2)}) collective-permute-start(bf16[2,512,512]{2,1,0:T(8,128)(2,1)S(1)} %collective-permute-done.rest_1_), channel_id=1, source_target_pairs={{0,1},{1,0},{2,3},{3,2},{4,5},{5,4},{6,7},{7,6},{8,9},{9,8},{10,11... | collective-permute-start | bytes 3145736 | tf_op jit(solution)/shard_map/cond/branch_0_fun/ppermute | solution.py:173
  74.0 34.3 %collective-permute-start.4 = (bf16[2,512,512]{2,1,0:T(8,128)(2,1)S(1)}, bf16[2,512,512]{2,1,0:T(8,128)(2,1)}, u32[]{:S(2)}, u32[]{:S(2)}) collective-permute-start(bf16[2,512,512]{2,1,0:T(8,128)(2,1)S(1)} %slice_bitcast_fusion.rest_0_), channel_id=1, source_target_pairs={{0,1},{1,0},{2,3},{3,2},{4,5},{5,4},{6,7},{7,6},{8,9},{9,8},{10,11... | collective-permute-start | bytes 3145736 | tf_op jit(solution)/shard_map/cond/branch_0_fun/ppermute | solution.py:173
  74.0 34.3 %collective-permute-start.6 = (bf16[2,512,512]{2,1,0:T(8,128)(2,1)S(1)}, bf16[2,512,512]{2,1,0:T(8,128)(2,1)}, u32[]{:S(2)}, u32[]{:S(2)}) collective-permute-start(bf16[2,512,512]{2,1,0:T(8,128)(2,1)S(1)} %collective-permute-done.1.rest_2_), channel_id=1, source_target_pairs={{0,1},{1,0},{2,3},{3,2},{4,5},{5,4},{6,7},{7,6},{8,9},{9,8},{10,11... | collective-permute-start | bytes 3145736 | tf_op jit(solution)/shard_map/cond/branch_0_fun/ppermute | solution.py:173
  106.0 2.3 collective-permute-start.9
  122.0 55.8 %all-to-all-start.3 = ((bf16[32,17,16,128]{3,2,1,0:T(8,128)(2,1)}), bf16[32,17,16,128]{3,2,1,0:T(8,128)(2,1)}, u32[]{:S(2)}, u32[]{:S(2)}) async-start(bf16[32,17,16,128]{3,2,1,0:T(8,128)(2,1)} %solve_0.5), calls=%async_computation.3 | async-start | bytes 4456448 | tf_op jit(solution)/shard_map/cond/branch_0_fun/all_to_all | solution.py:518
  128.9 33.0 %collective-permute-start.3 = (bf16[1,512,512]{2,1,0:T(8,128)(2,1)S(1)}, bf16[1,512,512]{2,1,0:T(8,128)(2,1)S(1)}, u32[]{:S(2)}, u32[]{:S(2)}) collective-permute-start(bf16[1,512,512]{2,1,0:T(8,128)(2,1)S(1)} %slice.31), channel_id=1, source_target_pairs={{0,2},{1,3},{2,0},{3,1},{4,6},{5,7},{6,4},{7,5},{8,10},{9,11},{10,... | collective-permute-start | bytes 1572872 | tf_op jit(solution)/shard_map/cond/branch_0_fun/ppermute | solution.py:173
  161.9 2.4 collective-permute-start.7
  177.8 55.8 %all-to-all-start.1 = ((bf16[32,17,16,128]{3,2,1,0:T(8,128)(2,1)}), bf16[32,17,16,128]{3,2,1,0:T(8,128)(2,1)S(1)}, u32[]{:S(2)}, u32[]{:S(2)}) async-start(bf16[32,17,16,128]{3,2,1,0:T(8,128)(2,1)} %solve_1.5), calls=%async_computation.1 | async-start | bytes 4456448 | tf_op jit(solution)/shard_map/cond/branch_0_fun/all_to_all | solution.py:518
  189.0 56.3 %collective-permute-start.10 = (bf16[1,544,128]{2,1,0:T(8,128)(2,1)}, bf16[1,544,128]{2,1,0:T(8,128)(2,1)S(1)}, u32[]{:S(2)}, u32[]{:S(2)}) collective-permute-start(bf16[1,544,128]{2,1,0:T(8,128)(2,1)} %get-tuple-element.88), channel_id=1, source_target_pairs={{0,1},{1,2},{2,3},{3,4},{4,5},{5,6},{6,7},{7,8},{8,9},{9,10},{10,1... | collective-permute-start | bytes 417800 | tf_op jit(solution)/shard_map/cond/branch_0_fun/ppermute | solution.py:513
  192.4 53.0 %collective-permute-start.11 = (bf16[1,544,128]{2,1,0:T(8,128)(2,1)}, bf16[1,544,128]{2,1,0:T(8,128)(2,1)S(1)}, u32[]{:S(2)}, u32[]{:S(2)}) collective-permute-start(bf16[1,544,128]{2,1,0:T(8,128)(2,1)} %get-tuple-element.89), channel_id=1, source_target_pairs={{1,0},{2,1},{3,2},{4,3},{5,4},{6,5},{7,6},{8,7},{9,8},{10,9},{11,1... | collective-permute-start | bytes 417800 | tf_op jit(solution)/shard_map/cond/branch_0_fun/ppermute | solution.py:513
  235.7 9.7 %collective-permute-start.12 = (bf16[1,544,128]{2,1,0:T(8,128)(2,1)S(1)}, bf16[1,544,128]{2,1,0:T(8,128)(2,1)S(1)}, u32[]{:S(2)}, u32[]{:S(2)}) collective-permute-start(bf16[1,544,128]{2,1,0:T(8,128)(2,1)S(1)} %get-tuple-element.90), channel_id=1, source_target_pairs={{0,1},{1,2},{2,3},{3,4},{4,5},{5,6},{6,7},{7,8},{8,9},{9,10},{10,1... | collective-permute-start | bytes 417800 | tf_op jit(solution)/shard_map/cond/branch_0_fun/ppermute | solution.py:513
  238.8 8.2 %collective-permute-start.13 = (bf16[1,544,128]{2,1,0:T(8,128)(2,1)S(1)}, bf16[1,544,128]{2,1,0:T(8,128)(2,1)S(1)}, u32[]{:S(2)}, u32[]{:S(2)}) collective-permute-start(bf16[1,544,128]{2,1,0:T(8,128)(2,1)S(1)} %get-tuple-element.91), channel_id=1, source_target_pairs={{1,0},{2,1},{3,2},{4,3},{5,4},{6,5},{7,6},{8,7},{9,8},{10,9},{11,1... | collective-permute-start | bytes 417800 | tf_op jit(solution)/shard_map/cond/branch_0_fun/ppermute | solution.py:513
